TPU v7x, 256 devices: a whole 4x4x8 slice. The times are simulated.
256 devices in a mesh: dp: 32 (over y, x, core), replica: 8 (over z).
Axes of the slice: x: 4, y: 4, z: 8, core: 2. Of those that a mesh axis runs over, the one named last changes fastest.
Arguments:
- grads: bfloat16 [1024, 256, 256], P('dp'), may hold values from -6 to 6
- owner: int32 [1024, 1], replicated, may hold values from 0 to 31; in each aligned block of 32 rows (0 to 31, 32 to 63, ...) at most 2 rows name the same one
- left_root: bfloat16 [32, 64, 256, 256], P('dp', None, 'replica'), may hold values from -0.375 to 0.375
- right_root: bfloat16 [32, 64, 256, 256], P('dp'), may hold values from -0.375 to 0.375
- first_moment: float32 [32, 64, 256, 256], P('dp', None, 'replica'), may hold values from -6 to 6
- second_moment: float32 [32, 64, 256, 256], P('dp', None, 'replica'), may hold values from 0.01 to 1
Outputs:
- update: bfloat16 [32, 64, 256, 256], P('dp')
Inputs may be any that keep to these rules, and one draw needn't show every extreme that they name: Among the 32 blocks of one flat shard (blocks s * 32 to s * 32 + 31) at most 2 name the same owner; some owner receives exactly 2 from some shard.
All inputs are finite; a program needn't handle non-finite values.
Results may differ from a plain program's by a relative error of at most 0.005.
Values may be sent and summed in bfloat16 or wider, within the bound.
A program may use at most 128 MiB of HBM per device.

v0:
```python
import jax
import jax.numpy as jnp
from jax import lax
from jax.sharding import PartitionSpec as P


def per_device(grads, owner, left_root, right_root, first_moment, second_moment):
    n_shards = lax.axis_size("dp")
    myself = lax.axis_index("dp")
    replica_idx = lax.axis_index("replica")
    per_shard = grads.shape[0]
    order = grads.shape[1]
    lroot = left_root[0]
    rroot = right_root[0]
    mone = first_moment[0]
    mtwo = second_moment[0]
    num_slots = lroot.shape[0]
    share = lroot.shape[1]
    per_pair = num_slots // n_shards
    owners = owner[:, 0]
    mine = lax.dynamic_slice_in_dim(owners, myself * per_shard, per_shard)
    equal = (mine[:, None] == mine[None, :]).astype(jnp.int32)
    earlier = (jnp.arange(per_shard)[None, :] < jnp.arange(per_shard)[:, None]).astype(jnp.int32)
    ranks = jnp.sum(equal * earlier, axis=1)
    target = mine * per_pair + ranks
    counts = jnp.sum((owners.reshape(n_shards, per_shard) == myself).astype(jnp.int32), axis=1)
    live = (jnp.arange(per_pair)[None, :] < counts[:, None]).astype(jnp.float32).reshape(num_slots)
    outgoing = jnp.zeros((num_slots, order, order), jnp.bfloat16).at[target].set(grads)
    incoming = lax.all_to_all(
        outgoing.reshape(n_shards, per_pair, order, order),
        "dp",
        split_axis=0,
        concat_axis=0,
        tiled=True,
    )
    received = incoming.reshape(num_slots, order, order)
    own_rows = lax.dynamic_slice_in_dim(received, replica_idx * share, share, 1)
    left = jnp.einsum("krc,kcd->krd", lroot, received, preferred_element_type=jnp.float32).astype(
        jnp.bfloat16
    )
    precond = jnp.einsum("krc,kcd->krd", left, rroot, preferred_element_type=jnp.float32)
    grad32 = own_rows.astype(jnp.float32)
    moment_one = 0.9 * mone + 0.1 * grad32
    moment_two = 0.999 * mtwo + 0.001 * grad32 * grad32
    adam = moment_one / (jnp.sqrt(moment_two) + 1e-08)
    sum_adam = jnp.sum(adam * adam, axis=(1, 2))
    sum_pre = jnp.sum(precond * precond, axis=(1, 2))
    total = float(order * order)
    whole_adam, whole_pre = lax.psum((sum_adam, sum_pre), "replica")
    scale = jnp.sqrt(whole_adam / total) / jnp.sqrt(whole_pre / total + 1e-06)
    finished = (precond * (live * scale)[:, None, None]).astype(jnp.bfloat16)
    result = lax.all_gather(finished, "replica", axis=1, tiled=True)
    return result[None]


def solution(mesh):
    placed = (
        P("dp", None, None),
        P(),
        P("dp", None, "replica", None),
        P("dp", None, None, None),
        P("dp", None, "replica", None),
        P("dp", None, "replica", None),
    )
    return jax.shard_map(
        per_device, mesh=mesh, in_specs=placed, out_specs=P("dp", None, None, None), check_vma=False
    )
```

profile of v0, /device:TPU:1, one launch (start us, length us, event | category | flops | bytes accessed | tf_op | source)
XLA Modules:
  0.0 274.8 jit_solution(455115881120370798)
XLA Ops:
  6.5 0.0 copy-start
  6.5 0.8 fusion.13
  7.4 0.2 select_reduce_fusion
  7.5 0.7 fusion.12
  8.3 4.4 %broadcast_in_dim.4 = bf16[64,256,256]{2,1,0:T(8,128)(2,1)} broadcast(bf16[]{:T(256)} %constant.18.clone.1), dimensions={} | broadcast | bytes 8388610 | tf_op jit(solution)/shard_map/broadcast_in_dim | solution.py:28
  12.7 11.2 %scatter_fusion = bf16[64,256,256]{2,1,0:T(8,128)(2,1)} fusion(bf16[64,256,256]{2,1,0:T(8,128)(2,1)} %broadcast_in_dim.4, s32[32]{0:T(128)S(1)} %fusion.12, bf16[32,256,256]{2,1,0:T(8,128)(2,1)} %param.6), kind=kCustom, calls=%fused_computation | custom fusion | bytes 12583040 | tf_op jit(solution)/shard_map/scatter | solution.py:28
  23.9 0.0 copy-start.1
  23.9 8.8 %all-to-all-start = ((bf16[32,2,256,256]{3,2,1,0:T(8,128)(2,1)}), bf16[32,2,256,256]{3,2,1,0:T(8,128)(2,1)}, u32[]{:S(2)}, u32[]{:S(2)}) async-start(bf16[32,2,256,256]{3,2,1,0:T(8,128)(2,1)} %bitcast.32), calls=%async_computation | async-start | bytes 16777216 | tf_op jit(solution)/shard_map/all_to_all | solution.py:29
  32.7 0.0 all-gather.2.cloned.1.call-start
  32.7 0.0 copy-done.1
  32.8 0.1 reshape.27
  32.9 0.1 reduce_sum.40
  33.0 0.1 iota_compare_fusion
  33.0 0.1 lt.52
  33.2 99.3 %all-to-all-done = bf16[32,2,256,256]{3,2,1,0:T(8,128)(2,1)} async-done(((bf16[32,2,256,256]{3,2,1,0:T(8,128)(2,1)}), bf16[32,2,256,256]{3,2,1,0:T(8,128)(2,1)}, u32[]{:S(2)}, u32[]{:S(2)}) %all-to-all-start) | async-done | bytes 8388640 | tf_op jit(solution)/shard_map/all_to_all | solution.py:29
  132.4 0.0 copy-done
  132.4 8.7 %multiply_reduce_fusion = (f32[64]{0:T(128)S(1)}, f32[64,32,256]{2,1,0:T(8,128)S(1)}) fusion(bf16[1,64,256,256]{3,2,1,0:T(8,128)(2,1)} %param.9, bf16[64,256,256]{2,1,0:T(8,128)(2,1)} %bitcast.4, bf16[1,64,32,256]{3,2,1,0:T(8,128)(2,1)S(1)} %copy-done), kind=kOutput, calls=%fused_computation.12 | convolution fusion | flops 538443712 | bytes 19923200 | tf_op jit(solution)/shard_map/krc,kcd->krd/dot_general | solution.py:41
  141.2 4.4 %fusion.8 = f32[64]{0:T(128)S(1)} fusion(f32[1,64,32,256]{3,2,1,0:T(8,128)} %param.11, f32[1,64,32,256]{3,2,1,0:T(8,128)} %param.10, bf16[64,256,256]{2,1,0:T(8,128)(2,1)} %bitcast.4, s32[]{:T(128)S(6)} %select_n.12), kind=kLoop, calls=%fused_computation.13 | loop fusion | flops 6291392 | bytes 5243140 | tf_op jit(solution)/shard_map/reduce_sum | solution.py:46
  145.5 16.2 %all-reduce = (f32[64]{0:T(128)S(1)}, f32[64]{0:T(128)S(1)}) all-reduce(f32[64]{0:T(128)S(1)} %get-tuple-element.7, f32[64]{0:T(128)S(1)} %fusion.8), channel_id=1, replica_groups=mesh['dp'=32,'replica'=8] {'replica'}, use_global_device_ids=true, to_apply=%region_6.0 | all-reduce | flops 128 | bytes 1024 | tf_op jit(solution)/shard_map/psum | solution.py:49
  161.8 1.2 multiply_convert_fusion
  162.9 0.0 all-gather.2.cloned.1.call-update
  162.9 97.3 %all-gather.2.cloned.1.call-done = bf16[64,256,256]{2,1,0:T(8,128)(2,1)} async-done(((bf16[64,32,256]{2,1,0:T(8,128)(2,1)}), bf16[64,256,256]{2,1,0:T(8,128)(2,1)}) %all-gather.2.cloned.1.call-update) | async-done | bytes 8388624 | tf_op jit(solution)/shard_map/all_gather | solution.py:52
  260.2 7.8 %copy.9 = bf16[1,64,256,256]{3,2,1,0:T(8,128)(2,1)} copy(bf16[1,64,256,256]{3,2,1,0:T(8,128)(2,1)} %bitcast.33) | data formatting | bytes 16777216
  (2 shorter events, 0.0 us)
Async XLA Ops:
  6.5 125.9 %copy-start = (bf16[1,64,32,256]{3,2,1,0:T(8,128)(2,1)S(1)}, bf16[1,64,32,256]{3,2,1,0:T(8,128)(2,1)}, u32[]{:S(2)}) copy-start(bf16[1,64,32,256]{3,2,1,0:T(8,128)(2,1)} %param.8) | copy-start | bytes 3145732
  23.9 8.8 %copy-start.1 = (s32[1024,1]{0,1:T(1,128)S(1)}, s32[1024,1]{0,1:T(1,128)}, u32[]{:S(2)}) copy-start(s32[1024,1]{0,1:T(1,128)} %param.7) | copy-start | bytes 12292
  23.9 108.5 %all-to-all-start = ((bf16[32,2,256,256]{3,2,1,0:T(8,128)(2,1)}), bf16[32,2,256,256]{3,2,1,0:T(8,128)(2,1)}, u32[]{:S(2)}, u32[]{:S(2)}) async-start(bf16[32,2,256,256]{3,2,1,0:T(8,128)(2,1)} %bitcast.32), calls=%async_computation | async-start | bytes 16777216 | tf_op jit(solution)/shard_map/all_to_all | solution.py:29
  32.7 227.5 %all-gather.2.cloned.1.call-start = ((), (), s32[]{:S(2)}) async-start(), calls=%async_computation.1 | async-start | bytes 9437184 | tf_op jit(solution)/shard_map/all_gather | solution.py:52
Sparse Core Ops, SparseCore 0:
  163.1 97.0 all-gather.1
where the time goes:
time: 275 us
  waiting for transfers between devices  197 us (72%)
  local copies, waits for them, and re-layouts  24.4 us (9%)
  blocking collectives  16.2 us (6%)
  between operations  13.4 us (5%)
  starting transfers between devices  8.82 us (3%)
  matrix products  8.73 us (3%)
  other arithmetic  6.65 us (2%)
    all_to_all x1, waiting for transfers between devices, per_device(): lax.all_to_all(outgoing.reshape(n_shards, per_pair, order, order), 'dp',...  99.3 us
    all_gather x1, waiting for transfers between devices, per_device(): result = lax.all_gather(finished, 'replica', axis=1, tiled=True)  97.3 us
    psum x1, blocking collectives, per_device(): whole_adam, whole_pre = lax.psum((sum_adam, sum_pre), 'replica')  16.2 us
    scatter x1, local copies, waits for them, and re-layouts, per_device(): jnp.zeros((num_slots, order, order), jnp.bfloat16).at[target].set(grads)  11.2 us
    all_to_all x1, starting transfers between devices, per_device(): lax.all_to_all(outgoing.reshape(n_shards, per_pair, order, order), 'dp',...  8.78 us
    dot_general x1, matrix products, per_device(): jnp.einsum('krc,kcd->krd', left, rroot, preferred_element_type=jnp.float32)  8.73 us
    unnamed x5, local copies, waits for them, and re-layouts  7.78 us
  transfers between devices with their start and end apart: 2, of which 2 were waited for; matrix products, arithmetic and copies ran while one was open for 0% of the time, Pallas kernels for 0%

commit v1 on v0

v1 whole, which is shorter than its diff:
```python
import functools

import jax
import jax.numpy as jnp
from jax import lax
from jax.experimental import pallas as pl
from jax.experimental.pallas import tpu as pltpu
from jax.sharding import PartitionSpec as P

MESH = pl.DeviceIdType.MESH
N_Y, N_X, N_C = 4, 4, 2
N_DP = N_Y * N_X * N_C
N_Z = 8
CHUNK = 8
RING = 4
SIGNS = (1, -1)
LIMIT = 50

START = (0, 12, 16, 40, 48, 60, 64)


def decode(kind, q):
    d, g = (lax.rem(q, 3), q // 3) if kind % 2 == 0 else (3, q)
    first = lax.rem(d + 3, 4)
    dc = lax.rem(g, 2)
    if kind < 2:
        half, second = g // 2, 0
    elif kind < 4:
        half, second = g // 4, 3 - 2 * lax.rem(g // 2, 2)
    else:
        half, second = g // 2, 2
    return half, first, second, dc


def step_kernel(
    owner, grads_hbm, left_hbm, right_hbm, mone_hbm, mtwo_hbm, recv_v, scale_out,
    grads_v, out_v, stage_v, pass_v, relay_v, left_v, right_v, mone_v, mtwo_v,
    adam_v, square_v, tiles_v, idx_v, idx,
    load_sems, left_sems, own_sems, idx_sem, send_sems, recv_sems, ring_send, ring_recv, zsend, zrecv,
):
    me, z = lax.axis_index("dp"), lax.axis_index("replica")
    per_shard, order = grads_hbm.shape[0], grads_hbm.shape[1]
    slots, share = mone_hbm.shape[0], mone_hbm.shape[1]
    total = float(order * order)
    per_ring = slots // RING
    y, x, c = me // (N_X * N_C), (me // N_C) % N_X, me % N_C

    def at(dy, dx, dc):
        return (
            lax.rem(y + dy + N_Y, N_Y) * (N_X * N_C) + lax.rem(x + dx + N_X, N_X) * N_C + lax.rem(c + dc, N_C)
        )

    def along(half, first, second, dc):
        return at(second + half * (first - second), first + half * (second - first), dc)

    def slot_of(kind, pos):
        half, first, second, dc = decode(kind, pos - START[kind])
        return 2 * along(half, first, second, dc) + half

    barrier = pltpu.get_barrier_semaphore()
    near = [(0, 0, 1)] + [(dy, dx, dc) for dy, dx in ((0, 1), (0, -1), (1, 0), (-1, 0)) for dc in range(N_C)]
    for step in near:
        pl.semaphore_signal(barrier, inc=1, device_id=(at(*step), z), device_id_type=MESH)
    for dz in range(1, N_Z):
        pl.semaphore_signal(barrier, inc=1, device_id=(me, lax.rem(z + dz, N_Z)), device_id_type=MESH)

    loads = [
        pltpu.make_async_copy(grads_hbm, grads_v.at[pl.ds(0, per_shard)], load_sems.at[0]),
        pltpu.make_async_copy(mone_hbm, mone_v, load_sems.at[1]),
        pltpu.make_async_copy(mtwo_hbm, mtwo_v, load_sems.at[2]),
        pltpu.make_async_copy(right_hbm, right_v, load_sems.at[3]),
    ]
    loads[0].start()
    for kind in range(6):

        def load_left(pos, carry):
            pltpu.make_async_copy(
                left_hbm.at[slot_of(kind, pos)], left_v.at[z, pos], left_sems.at[pos // per_ring]
            ).start()
            return carry

        lax.fori_loop(START[kind], START[kind + 1], load_left, 0)
    for load in loads[1:]:
        load.start()
    grads_v[per_shard] = jnp.zeros((order, order), jnp.bfloat16)

    row = lax.broadcasted_iota(jnp.int32, (per_shard, 128), 0)
    lane = lax.broadcasted_iota(jnp.int32, (per_shard, 128), 1)
    per_line = 128 // per_shard
    line = owner[:, pl.ds(pl.multiple_of(me // per_line * 128, 128), 128)]
    mine = pltpu.roll(
        jnp.broadcast_to(line, (per_shard, 128)), lax.rem(128 - lax.rem(me, per_line) * per_shard, 128), 1
    )
    names = jnp.sum(jnp.where(row == lane, mine, 0), axis=1, keepdims=True)
    ranks = jnp.sum(jnp.where((names == mine) & (lane < row), 1, 0), axis=1, keepdims=True)
    found = jnp.where(2 * names + ranks == lane, row - per_shard, 0)
    idx_v[...] = per_shard + jnp.sum(found, axis=0, keepdims=True)
    to_scalars = pltpu.make_async_copy(idx_v, idx, idx_sem)
    to_scalars.start()
    to_scalars.wait()
    loads[0].wait()
    pl.semaphore_wait(barrier, len(near) + N_Z - 1)

    def pack(half, first, part, into):
        def one(i, carry):
            p = along(half, first, i // N_C, lax.rem(i, N_C))
            into[i] = grads_v[idx[0, 2 * p + half]]
            return carry

        lax.fori_loop(4 * part, 4 * part + 4, one, 0)

    count = [0]

    def message(src, dst, target):
        n = count[0]
        count[0] += 1
        return pltpu.make_async_remote_copy(
            src_ref=src, dst_ref=dst, send_sem=send_sems.at[n], recv_sem=recv_sems.at[n],
            device_id=(target, z), device_id_type=MESH,
        )

    def place(kind, g):
        n = 1 if kind % 2 else 3
        return recv_v.at[pl.ds(START[kind] + n * g, n)]

    pieces = (pl.ds(0, 3), pl.ds(3, 1))
    via, straight, onward = {}, {}, {}
    far, ahead, inside, passed, own = {}, {}, {}, {}, {}
    for h in range(2):
        for part, sign in enumerate(SIGNS):
            half_part = pl.ds(4 * part, 4)
            via[h, part] = message(out_v.at[h, 2, half_part], pass_v.at[h, part], along(h, sign, 0, 0))
            straight[h, part] = message(out_v.at[h, part], stage_v.at[h, 2 * part], along(h, sign, 0, 0))
            onward[h, part] = message(pass_v.at[h, part], stage_v.at[h, 3, half_part], along(h, sign, 0, 0))
    for h in range(2):
        for m, piece in enumerate(pieces):
            for part, sign in enumerate(SIGNS):
                far[h, m, part] = message(
                    stage_v.at[h, piece, 4 + part], relay_v.at[h, part, piece], along(h, 0, sign, 0)
                )
                for dc in range(N_C):
                    ahead[h, m, part, dc] = message(
                        stage_v.at[h, piece, 2 * (sign % 4) + dc],
                        place(2 + m, (h * 2 + part) * 2 + dc),
                        along(h, 0, sign, dc),
                    )
                passed[h, m, part] = message(
                    relay_v.at[h, part, piece], place(4 + m, h * 2 + part), along(h, 0, sign, part)
                )
            inside[h, m] = message(stage_v.at[h, piece, 1], place(m, h * 2 + 1), at(0, 0, 1))
            own[h, m] = pltpu.make_async_copy(stage_v.at[h, piece, 0], place(m, h * 2), own_sems.at[h, m])

    def ring(part, t, chunk, source):
        piece = left_v.at[source, pl.ds(chunk * per_ring, per_ring)]
        return pltpu.make_async_remote_copy(
            src_ref=piece, dst_ref=piece,
            send_sem=ring_send.at[part, t, chunk], recv_sem=ring_recv.at[part, t, chunk],
            device_id=(me, lax.rem(z + SIGNS[part] + N_Z, N_Z)), device_id_type=MESH,
        )

    def ring_out(part, t, chunk):
        return ring(part, t, chunk, lax.rem(z - SIGNS[part] * t + N_Z, N_Z))

    def ring_in(part, t, chunk):
        return ring(part, t, chunk, lax.rem(z - SIGNS[part] * (t + 1) + N_Z, N_Z))

    def travels(part, t, chunk):
        return t < 3 or chunk % 2 == part

    def pass_on(t, *chunks):
        for chunk in chunks:
            for part in range(2):
                if travels(part, t, chunk):
                    ring_in(part, t, chunk).wait_recv()
                if t < 3 and travels(part, t + 1, chunk):
                    ring_out(part, t + 1, chunk).start()

    rows = pl.ds(pl.multiple_of(z * share, share), share)

    def fold(values):
        values = values[:, :128] + values[:, 128:]
        return jnp.sum(values.reshape(values.shape[0] // 8, 8, 128), axis=0)

    def adam(kind):
        def one(pos, carry):
            k = slot_of(kind, pos)
            grad32 = recv_v[pos, rows, :].astype(jnp.float32)
            moment_one = 0.9 * mone_v[k] + 0.1 * grad32
            moment_two = 0.999 * mtwo_v[k] + 0.001 * grad32 * grad32
            ratio = moment_one / (jnp.sqrt(moment_two) + 1e-08)
            adam_v[k] = fold(ratio * ratio)
            return carry

        lax.fori_loop(START[kind], START[kind + 1], one, 0)

    def multiply(kind, begin, end):
        def some(i, carry):
            places = [begin + 4 * i + j for j in range(4)]
            ks = [slot_of(kind, pos) for pos in places]
            halves = [
                jnp.dot(
                    left_v[:, pos].reshape(order, order), recv_v[pos], preferred_element_type=jnp.float32
                ).astype(jnp.bfloat16)
                for pos in places
            ]
            for pos, k, half in zip(places, ks, halves):
                precond = jnp.dot(half, right_v[k], preferred_element_type=jnp.float32)
                square_v[k] = fold(precond * precond)
                recv_v[pos] = precond.astype(jnp.bfloat16)
            return carry

        lax.fori_loop(0, (end - begin) // 4, some, 0)

    def by_lane(sums):
        by_slot = jnp.sum(jnp.sum(sums, axis=1), axis=1, keepdims=True)
        spread = jnp.broadcast_to(by_slot, (slots, 128))
        return jnp.sum(jnp.where(diagonal, spread, 0.0), axis=0, keepdims=True)

    diagonal = lax.broadcasted_iota(jnp.int32, (slots, 128), 0) == lax.broadcasted_iota(
        jnp.int32, (slots, 128), 1
    )

    for h in range(2):
        for part in range(2):
            pack(h, 2, part, out_v.at[h, 2])
            via[h, part].start()
    for chunk in range(RING):
        first = pl.ds(chunk * per_ring, per_ring)
        pltpu.make_async_copy(left_hbm.at[first], left_v.at[z, first], left_sems.at[chunk]).wait()
        for part in range(2):
            ring_out(part, 0, chunk).start()
    for h in range(2):
        for part, sign in enumerate(SIGNS):
            for half_part in range(2):
                pack(h, sign, half_part, out_v.at[h, part])
            straight[h, part].start()
    for h in range(2):
        for half_part in range(2):
            pack(h, 0, half_part, stage_v.at[h, 1])

    pass_on(0, 0)
    for h in range(2):
        for part in range(2):
            via[h, part].wait_recv()
            onward[h, part].start()
    pass_on(0, 1, 2, 3)
    pass_on(1, 0)
    for load in loads[1:]:
        load.wait()
    for m in range(2):
        for h in range(2):
            for part in range(2):
                (straight if m == 0 else onward)[h, part].wait_recv()
            for part in range(2):
                far[h, m, part].start()
            for part in range(2):
                for dc in range(N_C):
                    ahead[h, m, part, dc].start()
            inside[h, m].start()
            own[h, m].start()
        pass_on(1, *((1, 2) if m == 0 else (3,)))
    for m in range(2):
        for h in range(2):
            own[h, m].wait()
            inside[h, m].wait_recv()
        adam(m)
    pass_on(2, 0)
    for h in range(2):
        for part in range(2):
            far[h, 0, part].wait_recv()
            passed[h, 0, part].start()
    pass_on(2, 1, 2, 3)
    for m in range(2):
        for h in range(2):
            for part in range(2):
                if m == 1:
                    far[h, m, part].wait_recv()
                    passed[h, m, part].start()
                for dc in range(N_C):
                    ahead[h, m, part, dc].wait_recv()
        adam(2 + m)
        if m == 0:
            pass_on(3, 0, 1)
            multiply(0, 0, 12)
            multiply(1, 12, 16)
            multiply(2, 16, 32)
    pass_on(3, 2, 3)
    multiply(2, 32, 40)
    multiply(3, 40, 48)
    for m in range(2):
        for h in range(2):
            for part in range(2):
                passed[h, m, part].wait_recv()
        adam(4 + m)
        if m == 0:
            multiply(4, 48, 60)

    tiles_v[0] = jnp.broadcast_to(by_lane(adam_v[...]), (8, 128))

    def tell(dz):
        return pltpu.make_async_remote_copy(
            src_ref=tiles_v.at[0],
            dst_ref=tiles_v.at[dz],
            send_sem=zsend.at[dz],
            recv_sem=zrecv.at[dz],
            device_id=(me, lax.rem(z + dz, N_Z)),
            device_id_type=MESH,
        )

    for dz in range(1, N_Z):
        tell(dz).start()
    multiply(5, 60, 64)
    sum_pre = by_lane(square_v[...])
    for group in (via, straight, onward, far, ahead, inside, passed):
        for copy in group.values():
            copy.wait_send()
    for t in range(4):
        for chunk in range(RING):
            for part in range(2):
                if travels(part, t, chunk):
                    ring_out(part, t, chunk).wait_send()
    for dz in range(1, N_Z):
        tell(dz).wait()
    sum_adam = jnp.sum(tiles_v[...], axis=0)[:1]
    shard = lax.broadcasted_iota(jnp.int32, (owner.shape[1], 128), 0) // per_shard
    slot = lax.broadcasted_iota(jnp.int32, (owner.shape[1], 128), 1)
    ours = jnp.broadcast_to(jnp.where(owner[...] == me, 1.0, 0.0), (8, owner.shape[1]))
    counts = jnp.dot(
        ours.astype(jnp.bfloat16),
        jnp.where(shard == slot // 2, 1.0, 0.0).astype(jnp.bfloat16),
        preferred_element_type=jnp.float32,
    )[:1]
    rank = lax.rem(slot[:1], 2).astype(jnp.float32)
    live = jnp.where(counts > rank, 1.0, 0.0)
    scale = live * (jnp.sqrt(sum_adam / total) / jnp.sqrt(sum_pre / total + 1e-06))
    by_row = jnp.where(diagonal, jnp.broadcast_to(scale, (slots, 128)), 0.0)
    scale_out[...] = jnp.broadcast_to(jnp.sum(by_row, axis=1, keepdims=True), (slots, 128))


def step(owner, grads, left, right, mone, mtwo):
    per_shard, order, _ = grads.shape
    slots, share, _ = mone.shape
    block = (order, order)
    anywhere = pl.BlockSpec(memory_space=pl.ANY)
    vmem = pl.BlockSpec(memory_space=pltpu.VMEM)
    dma = pltpu.SemaphoreType.DMA
    return pl.pallas_call(
        step_kernel,
        out_shape=(
            pltpu.VMEM((slots, *block), jnp.bfloat16),
            pltpu.VMEM((slots, 128), jnp.float32),
        ),
        in_specs=[vmem] + [anywhere] * 5,
        out_specs=(vmem, vmem),
        scratch_shapes=[
            pltpu.VMEM((per_shard + 1, *block), jnp.bfloat16),
            pltpu.VMEM((2, 3, 8, *block), jnp.bfloat16),
            pltpu.VMEM((2, 4, 8, *block), jnp.bfloat16),
            pltpu.VMEM((2, 2, 4, *block), jnp.bfloat16),
            pltpu.VMEM((2, 2, 4, *block), jnp.bfloat16),
            pltpu.VMEM((N_Z, slots, share, order), jnp.bfloat16),
            pltpu.VMEM((slots, *block), jnp.bfloat16),
            pltpu.VMEM((slots, share, order), jnp.float32),
            pltpu.VMEM((slots, share, order), jnp.float32),
            pltpu.VMEM((slots, 8, 128), jnp.float32),
            pltpu.VMEM((slots, 8, 128), jnp.float32),
            pltpu.VMEM((N_Z, 8, 128), jnp.float32),
            pltpu.VMEM((1, 128), jnp.int32),
            pltpu.SMEM((1, 128), jnp.int32),
            dma((4,)),
            dma((RING,)),
            dma((2, 2)),
            dma,
            dma((48,)),
            dma((48,)),
            dma((2, 4, RING)),
            dma((2, 4, RING)),
            dma((N_Z,)),
            dma((N_Z,)),
        ],
        compiler_params=pltpu.CompilerParams(
            collective_id=0, has_side_effects=True, vmem_limit_bytes=LIMIT * 2**20
        ),
        cost_estimate=pl.CostEstimate(
            flops=4 * slots * order**3, bytes_accessed=4 * 10**8, transcendentals=10**6
        ),
    )(owner, grads, left, right, mone, mtwo)


def place_of(me, slot):
    y, x, c = me // (N_X * N_C), (me // N_C) % N_X, me % N_C
    source, half = slot // 2, lax.rem(slot, 2)
    dy = lax.rem(source // (N_X * N_C) - y + N_Y, N_Y)
    dx = lax.rem(lax.rem(source // N_C, N_X) - x + N_X, N_X)
    dc = lax.rem(source + c, N_C)
    first, second = dx + half * (dy - dx), dy + half * (dx - dy)
    d = lax.rem(first + 1, 4)
    g = half * 2 + dc
    beside = (half * 2 + (3 - second) // 2) * 2 + dc
    near = jnp.where(d == 3, START[1] + g, START[0] + 3 * g + d)
    middle = jnp.where(d == 3, START[3] + beside, START[2] + 3 * beside + d)
    away = jnp.where(d == 3, START[5] + g, START[4] + 3 * g + d)
    return jnp.where(second == 0, near, jnp.where(second == 2, away, middle))


def scale_kernel(x, scale, out):
    me, base = lax.axis_index("dp"), pl.program_id(0) * CHUNK
    for k in range(CHUNK):
        row = scale[k : k + 1, :]
        factor = jnp.concatenate([row, row], axis=1)
        out[k] = (x[place_of(me, base + k)].astype(jnp.float32) * factor).astype(jnp.bfloat16)


def apply_scale(x, scale):
    slots, order, _ = x.shape
    return pl.pallas_call(
        scale_kernel,
        grid=(slots // CHUNK,),
        out_shape=jax.ShapeDtypeStruct(x.shape, jnp.bfloat16),
        in_specs=[pl.BlockSpec(memory_space=pltpu.VMEM), pl.BlockSpec((CHUNK, 128), lambda i: (i, 0))],
        out_specs=pl.BlockSpec((CHUNK, order, order), lambda i: (i, 0, 0)),
        compiler_params=pltpu.CompilerParams(vmem_limit_bytes=24 * 2**20),
    )(x, scale)


def per_device(grads, owner, left_root, right_root, first_moment, second_moment):
    x, scale = step(
        owner.reshape(1, -1), grads, left_root[0], right_root[0], first_moment[0], second_moment[0]
    )
    return apply_scale(x, scale)[None]


def solution(mesh):
    placed = (
        P("dp", None, None),
        P(),
        P("dp", None, "replica", None),
        P("dp", None, None, None),
        P("dp", None, "replica", None),
        P("dp", None, "replica", None),
    )
    return jax.shard_map(
        per_device, mesh=mesh, in_specs=placed, out_specs=P("dp", None, None, None), check_vma=False
    )
```

time: 275 us -> 114 us (0.41)
  waiting for transfers between devices: 197 us -> 0 us
  Pallas kernels: 0 us -> 114 us
  local copies, waits for them, and re-layouts: 24.4 us -> 0 us
  blocking collectives: 16.2 us -> 0 us
  between operations: 13.4 us -> 0.01 us
  starting transfers between devices: 8.82 us -> 0 us
  matrix products: 8.73 us -> 0 us
  other arithmetic: 6.65 us -> 0 us
    pallas_call x0 -> x2, Pallas kernels: none -> 114 us  [the longest x1 108 us: step(): pl.pallas_call(step_kernel, out_shape=(pltpu.VMEM((slots, *block), jnp.bf...]
    all_to_all x1 -> x0, waiting for transfers between devices: 99.3 us -> none  [per_device(): lax.all_to_all(outgoing.reshape(n_shards, per_pair, order, order), 'dp',...]
    all_gather x1 -> x0, waiting for transfers between devices: 97.3 us -> none  [per_device(): result = lax.all_gather(finished, 'replica', axis=1, tiled=True)]
    psum x1 -> x0, blocking collectives: 16.2 us -> none  [per_device(): whole_adam, whole_pre = lax.psum((sum_adam, sum_pre), 'replica')]
    scatter x1 -> x0, local copies, waits for them, and re-layouts: 11.2 us -> none  [per_device(): jnp.zeros((num_slots, order, order), jnp.bfloat16).at[target].set(grads)]
    all_to_all x1 -> x0, starting transfers between devices: 8.78 us -> none  [per_device(): lax.all_to_all(outgoing.reshape(n_shards, per_pair, order, order), 'dp',...]
    dot_general x1 -> x0, matrix products: 8.73 us -> none  [per_device(): jnp.einsum('krc,kcd->krd', left, rroot, preferred_element_type=jnp.float32)]
    unnamed x5 -> x0, local copies, waits for them, and re-layouts: 7.78 us -> none
  transfers between devices with their start and end apart: 2 -> 0, of which waited for: 2 -> 0; matrix products, arithmetic and copies ran while one was open for 0% -> 0% of each run, Pallas kernels for 0% -> 0%
where the time goes in v1:
time: 114 us
  Pallas kernels  114 us (100%)
    pallas_call x1, Pallas kernels, step(): pl.pallas_call(step_kernel, out_shape=(pltpu.VMEM((slots, *block), jnp.bf...  108 us
    pallas_call x1, Pallas kernels, apply_scale(): pl.pallas_call(scale_kernel, grid=(slots // CHUNK,), out_shape=jax.ShapeD...  5.35 us

profile of v1, /device:TPU:1, one launch (start us, length us, event | category | flops | bytes accessed | tf_op | source)
XLA Modules:
  0.0 113.8 jit_solution(4070805305674336806)
XLA Ops:
  0.0 108.5 %shard_map.64 = (bf16[64,256,256]{2,1,0:T(8,128)(2,1)S(1)}, f32[64,128]{1,0:T(8,128)S(1)}) custom-call(s32[1,1024]{1,0:T(1,128)} %bitcast.10, bf16[32,256,256]{2,1,0:T(8,128)(2,1)} %grads_hbm.1, bf16[64,32,256]{2,1,0:T(8,128)(2,1)} %bitcast.9, bf16[64,256,256]{2,1,0:T(8,128)(2,1)} %bitcast.6, f32[64,32,256]{2,1,0:T(8,128)} %bitcast.7, f32[64,32,256]{2,1,0:T(8,128)} %bitcast.8), custom_call_target="tpu_custom_call" | custom-call | flops 4294967296 | bytes 400000000 | tf_op jit(solution)/shard_map/pallas_call | solution.py:347
  108.5 5.3 %shard_map.65 = bf16[64,256,256]{2,1,0:T(8,128)(2,1)} custom-call(bf16[64,256,256]{2,1,0:T(8,128)(2,1)S(1)} %get-tuple-element.7.x, f32[64,128]{1,0:T(8,128)S(1)} %get-tuple-element.8.scale), custom_call_target="tpu_custom_call" | custom-call | tf_op jit(solution)/shard_map/pallas_call | solution.py:416

commit v2 on v1

v2 whole, which is shorter than its diff:
```python
import functools

import jax
import jax.numpy as jnp
from jax import lax
from jax.experimental import pallas as pl
from jax.experimental.pallas import tpu as pltpu
from jax.sharding import PartitionSpec as P

MESH = pl.DeviceIdType.MESH
N_Y, N_X, N_C = 4, 4, 2
N_DP = N_Y * N_X * N_C
N_Z = 8
GROUP = 4
RING = 4
SIGNS = (1, -1)
LIMIT = 50

NEAR, NEAR_LONG, BESIDE, AWAY_LONG, AWAY, BESIDE_CROSS, BESIDE_LONG = range(7)
START = (0, 12, 16, 28, 32, 44, 56, 64)
PACKED = ((0, 0), (0, 1), (1, 0), (2, 0), (2, 1), (1, 1), (3, 0), (3, 1))
FULL = (pl.ds(0, 3), pl.ds(5, 3))


def decode(kind, q):
    long = kind in (NEAR_LONG, AWAY_LONG, BESIDE_LONG)
    d, g = (3, q) if long else (lax.rem(q, 3), q // 3)
    first, low = lax.rem(d + 3, 4), lax.rem(g, 2)
    if kind in (NEAR, NEAR_LONG):
        return g // 2, first, 0, low
    if kind in (AWAY, AWAY_LONG):
        return g // 2, first, 2, low
    return lax.rem(g // 2, 2), first, 3 - 2 * low, g // 4 if kind == BESIDE_LONG else int(kind == BESIDE_CROSS)


def step_kernel(
    owner, grads_hbm, left_hbm, right_hbm, mone_hbm, mtwo_hbm, recv_v, scale_out,
    grads_v, out_v, stage_v, pass_v, relay_v, left_v, right_v, mone_v, mtwo_v,
    adam_v, square_v, tiles_v, live_v, idx_v, idx,
    load_sems, left_sems, own_sems, idx_sem, send_sems, recv_sems, ring_send, ring_recv, zsend, zrecv,
):
    me, z = lax.axis_index("dp"), lax.axis_index("replica")
    per_shard, order = grads_hbm.shape[0], grads_hbm.shape[1]
    slots, share = mone_hbm.shape[0], mone_hbm.shape[1]
    total = float(order * order)
    per_ring = slots // RING
    y, x, c = me // (N_X * N_C), (me // N_C) % N_X, me % N_C

    def at(dy, dx, dc):
        return (
            lax.rem(y + dy + N_Y, N_Y) * (N_X * N_C) + lax.rem(x + dx + N_X, N_X) * N_C + lax.rem(c + dc, N_C)
        )

    def along(half, first, second, dc):
        return at(second + half * (first - second), first + half * (second - first), dc)

    def slot_of(kind, pos):
        half, first, second, dc = decode(kind, pos - START[kind])
        return 2 * along(half, first, second, dc) + half

    barrier = pltpu.get_barrier_semaphore()
    near = [(0, 0, 1)] + [(dy, dx, dc) for dy, dx in ((0, 1), (0, -1), (1, 0), (-1, 0)) for dc in range(N_C)]
    for step in near:
        pl.semaphore_signal(barrier, inc=1, device_id=(at(*step), z), device_id_type=MESH)
    for dz in range(1, N_Z):
        pl.semaphore_signal(barrier, inc=1, device_id=(me, lax.rem(z + dz, N_Z)), device_id_type=MESH)

    loads = [
        pltpu.make_async_copy(grads_hbm, grads_v.at[pl.ds(0, per_shard)], load_sems.at[0]),
        pltpu.make_async_copy(mone_hbm, mone_v, load_sems.at[1]),
        pltpu.make_async_copy(mtwo_hbm, mtwo_v, load_sems.at[2]),
        pltpu.make_async_copy(right_hbm, right_v, load_sems.at[3]),
    ]
    loads[0].start()
    row = lax.broadcasted_iota(jnp.int32, (per_shard, 128), 0)
    lane = lax.broadcasted_iota(jnp.int32, (per_shard, 128), 1)
    per_line = 128 // per_shard
    line = owner[:, pl.ds(pl.multiple_of(me // per_line * 128, 128), 128)]
    mine = pltpu.roll(
        jnp.broadcast_to(line, (per_shard, 128)), lax.rem(128 - lax.rem(me, per_line) * per_shard, 128), 1
    )
    names = jnp.sum(jnp.where(row == lane, mine, 0), axis=1, keepdims=True)
    ranks = jnp.sum(jnp.where((names == mine) & (lane < row), 1, 0), axis=1, keepdims=True)
    found = jnp.where(2 * names + ranks == lane, row - per_shard, 0)
    idx_v[...] = per_shard + jnp.sum(found, axis=0, keepdims=True)
    to_scalars = pltpu.make_async_copy(idx_v, idx, idx_sem)
    to_scalars.start()
    for kind in range(7):

        def load_left(pos, carry):
            pltpu.make_async_copy(
                left_hbm.at[slot_of(kind, pos)], left_v.at[z, pos], left_sems.at[pos // per_ring]
            ).start()
            return carry

        lax.fori_loop(START[kind], START[kind + 1], load_left, 0)
    for load in loads[1:]:
        load.start()
    grads_v[per_shard] = jnp.zeros((order, order), jnp.bfloat16)
    to_scalars.wait()
    loads[0].wait()
    pl.semaphore_wait(barrier, len(near) + N_Z - 1)

    def pack(half, first, places, into):
        for i in places:
            p = along(half, first, *PACKED[i])
            into[i] = grads_v[idx[0, 2 * p + half]]

    count = [0]

    def message(src, dst, target, plane=z):
        n = count[0]
        count[0] += 1
        return pltpu.make_async_remote_copy(
            src_ref=src, dst_ref=dst, send_sem=send_sems.at[n], recv_sem=recv_sems.at[n],
            device_id=(target, plane), device_id_type=MESH,
        )

    def place(kind, g):
        n = 1 if kind in (NEAR_LONG, AWAY_LONG, BESIDE_LONG) else 3
        return recv_v.at[pl.ds(START[kind] + n * g, n)]

    parity = lax.rem(z, 2)
    half_rows = pl.ds(pl.multiple_of(parity * (order // 2), order // 2), order // 2)
    other_rows = pl.ds(pl.multiple_of((1 - parity) * (order // 2), order // 2), order // 2)
    pieces = (pl.ds(0, 3), pl.ds(3, 1))
    via, straight, onward = {}, {}, {}
    far, ahead, inside, passed, own, swap, swapped = {}, {}, {}, {}, {}, {}, {}
    for h in range(2):
        for part, sign in enumerate(SIGNS):
            there = along(h, sign, 0, 0)
            straight[h, part] = message(out_v.at[h, part], stage_v.at[h, 2 * part], there)
            via[h, 0, part] = message(out_v.at[h, 2, FULL[part]], pass_v.at[h, part, pl.ds(0, 3)], there)
            onward[h, 0, part] = message(pass_v.at[h, part, pl.ds(0, 3)], stage_v.at[h, 3, FULL[part]], there)
            via[h, 1, part] = message(
                out_v.at[h, 2, 3 + part, half_rows], pass_v.at[h, part, 3, half_rows], there
            )
            onward[h, 1, part] = message(
                pass_v.at[h, part, 3, half_rows], stage_v.at[h, 3, 3 + part, half_rows], there
            )
            there = along(h, 0, sign, 0)
            last = along(h, 0, sign, part)
            far[h, 0, part] = message(
                stage_v.at[h, pieces[0], 3 + part], relay_v.at[h, part, pieces[0]], there
            )
            passed[h, 0, part] = message(relay_v.at[h, part, pieces[0]], place(AWAY, h * 2 + part), last)
            far[h, 1, part] = message(
                stage_v.at[h, 3, 3 + part, half_rows], relay_v.at[h, part, 3, half_rows], there
            )
            passed[h, 1, part] = message(
                relay_v.at[h, part, 3, half_rows], recv_v.at[START[AWAY_LONG] + h * 2 + part, half_rows], last
            )
            for m, piece in enumerate(pieces):
                for dc in range(N_C):
                    ahead[h, m, part, dc] = message(
                        stage_v.at[h, piece, PACKED.index((sign % 4, dc))],
                        place((BESIDE, BESIDE_CROSS)[dc], h * 2 + part) if m == 0 else place(BESIDE_LONG, dc * 4 + h * 2 + part),
                        along(h, 0, sign, dc),
                    )
        for m, piece in enumerate(pieces):
            inside[h, m] = message(stage_v.at[h, piece, 1], place((NEAR, NEAR_LONG)[m], h * 2 + 1), at(0, 0, 1))
            own[h, m] = pltpu.make_async_copy(stage_v.at[h, piece, 0], place((NEAR, NEAR_LONG)[m], h * 2), own_sems.at[h, m])
        step = (1 - 2 * parity) * (1 - 2 * h)
        plane = lax.rem(z + step + N_Z, N_Z)
        both = pl.ds(START[AWAY_LONG] + h * 2, 2)
        swap[h] = message(recv_v.at[both, half_rows], recv_v.at[both, half_rows], me, plane)
        swapped[h] = pltpu.make_async_remote_copy(
            src_ref=recv_v.at[both, other_rows], dst_ref=recv_v.at[both, other_rows],
            send_sem=send_sems.at[count[0] - 1], recv_sem=recv_sems.at[count[0] - 1],
            device_id=(me, plane), device_id_type=MESH,
        )

    def ring(part, t, chunk, source):
        piece = left_v.at[source, pl.ds(chunk * per_ring, per_ring)]
        return pltpu.make_async_remote_copy(
            src_ref=piece, dst_ref=piece,
            send_sem=ring_send.at[part, t, chunk], recv_sem=ring_recv.at[part, t, chunk],
            device_id=(me, lax.rem(z + SIGNS[part] + N_Z, N_Z)), device_id_type=MESH,
        )

    def ring_out(part, t, chunk):
        return ring(part, t, chunk, lax.rem(z - SIGNS[part] * t + N_Z, N_Z))

    def ring_in(part, t, chunk):
        return ring(part, t, chunk, lax.rem(z - SIGNS[part] * (t + 1) + N_Z, N_Z))

    def travels(part, t, chunk):
        return t < 3 or chunk % 2 == part

    def pass_on(t, *chunks):
        for chunk in chunks:
            for part in range(2):
                if travels(part, t, chunk):
                    ring_in(part, t, chunk).wait_recv()
                if t < 3 and travels(part, t + 1, chunk):
                    ring_out(part, t + 1, chunk).start()

    def begin(chunk):
        for part in range(2):
            ring_out(part, 0, chunk).start()

    rows = pl.ds(pl.multiple_of(z * share, share), share)

    def fold(values):
        values = values[:, :128] + values[:, 128:]
        return jnp.sum(values.reshape(values.shape[0] // 8, 8, 128), axis=0)

    def adam(kind):
        def some(i, carry):
            for j in range(4):
                pos = START[kind] + 4 * i + j
                k = slot_of(kind, pos)
                grad32 = recv_v[pos, rows, :].astype(jnp.float32)
                moment_one = 0.9 * mone_v[k] + 0.1 * grad32
                moment_two = 0.999 * mtwo_v[k] + 0.001 * grad32 * grad32
                ratio = moment_one / (jnp.sqrt(moment_two) + 1e-08)
                adam_v[k] = fold(ratio * ratio)
            return carry

        lax.fori_loop(0, (START[kind + 1] - START[kind]) // 4, some, 0)

    def multiply(kind):
        def some(i, carry):
            places = [START[kind] + 4 * i + j for j in range(4)]
            ks = [slot_of(kind, pos) for pos in places]
            halves = [
                jnp.dot(
                    left_v[:, pos].reshape(order, order), recv_v[pos], preferred_element_type=jnp.float32
                ).astype(jnp.bfloat16)
                for pos in places
            ]
            for pos, k, half in zip(places, ks, halves):
                precond = jnp.dot(half, right_v[k], preferred_element_type=jnp.float32)
                square_v[k] = fold(precond * precond)
                recv_v[pos] = precond.astype(jnp.bfloat16)
            return carry

        lax.fori_loop(0, (START[kind + 1] - START[kind]) // 4, some, 0)

    def count_live():
        shard = lax.broadcasted_iota(jnp.int32, (owner.shape[1], 128), 0) // per_shard
        slot = lax.broadcasted_iota(jnp.int32, (owner.shape[1], 128), 1)
        ours = jnp.broadcast_to(jnp.where(owner[...] == me, 1.0, 0.0), (8, owner.shape[1]))
        counts = jnp.dot(
            ours.astype(jnp.bfloat16),
            jnp.where(shard == slot // 2, 1.0, 0.0).astype(jnp.bfloat16),
            preferred_element_type=jnp.float32,
        )[:1]
        rank = lax.rem(slot[:1], 2).astype(jnp.float32)
        live_v[...] = jnp.where(counts > rank, 1.0, 0.0)

    def by_lane(sums):
        by_slot = jnp.sum(jnp.sum(sums, axis=1), axis=1, keepdims=True)
        spread = jnp.broadcast_to(by_slot, (slots, 128))
        return jnp.sum(jnp.where(diagonal, spread, 0.0), axis=0, keepdims=True)

    diagonal = lax.broadcasted_iota(jnp.int32, (slots, 128), 0) == lax.broadcasted_iota(
        jnp.int32, (slots, 128), 1
    )

    every = [(h, part) for h in range(2) for part in range(2)]
    for h, part in every:
        pack(h, 2, (3 + part,), out_v.at[h, 2])
        via[h, 1, part].start()
    for h, part in every:
        pack(h, 2, ((0, 1, 2), (5, 6, 7))[part], out_v.at[h, 2])
        via[h, 0, part].start()
    for chunk in range(RING):
        first = pl.ds(chunk * per_ring, per_ring)
        pltpu.make_async_copy(left_hbm.at[first], left_v.at[z, first], left_sems.at[chunk]).wait()
        if chunk < 2:
            begin(chunk)
    for h, part in every:
        pack(h, SIGNS[part], range(8), out_v.at[h, part])
        straight[h, part].start()
    for h, part in every:
        via[h, 1, part].wait_recv()
        onward[h, 1, part].start()
    for h in range(2):
        pack(h, 0, range(8), stage_v.at[h, 1])

    pass_on(0, 0)
    for h, part in every:
        onward[h, 1, part].wait_recv()
        far[h, 1, part].start()
    pass_on(0, 1)
    for h, part in every:
        via[h, 0, part].wait_recv()
        onward[h, 0, part].start()
    for h, part in every:
        far[h, 1, part].wait_recv()
        passed[h, 1, part].start()
    pass_on(1, 0)
    for h in range(2):
        for part in range(2):
            passed[h, 1, part].wait_recv()
        swap[h].start()
    pass_on(1, 1)
    begin(2)
    for load in loads[1:]:
        load.wait()
    count_live()
    pass_on(2, 0)
    for h, part in every:
        straight[h, part].wait_recv()
    for h, part in every:
        far[h, 0, part].start()
    for h in range(2):
        inside[h, 0].start()
        own[h, 0].start()
    pass_on(2, 1)
    begin(3)
    for h, part in every:
        ahead[h, 0, part, 0].start()
    for h in range(2):
        swapped[h].wait_recv()
        swap[h].wait_send()
    adam(AWAY_LONG)
    pass_on(0, 2)
    for h, part in every:
        onward[h, 0, part].wait_recv()
    for h in range(2):
        inside[h, 1].start()
        own[h, 1].start()
    pass_on(3, 0, 1)
    multiply(AWAY_LONG)
    pass_on(0, 3)
    for m in range(2):
        for h in range(2):
            own[h, m].wait()
            inside[h, m].wait_recv()
        adam((NEAR, NEAR_LONG)[m])
    for h, part in every:
        far[h, 0, part].wait_recv()
        passed[h, 0, part].start()
    multiply(NEAR)
    pass_on(1, 2)
    multiply(NEAR_LONG)
    for h, part in every:
        ahead[h, 0, part, 0].wait_recv()
    for h, part in every:
        ahead[h, 0, part, 1].start()
    pass_on(1, 3)
    adam(BESIDE)
    multiply(BESIDE)
    pass_on(2, 2)
    for h, part in every:
        passed[h, 0, part].wait_recv()
    for dc in range(N_C):
        for h, part in every:
            ahead[h, 1, part, dc].start()
    adam(AWAY)
    pass_on(2, 3)
    pass_on(3, 2)
    multiply(AWAY)
    for h, part in every:
        ahead[h, 0, part, 1].wait_recv()
    adam(BESIDE_CROSS)
    pass_on(3, 3)
    multiply(BESIDE_CROSS)
    for dc in range(N_C):
        for h, part in every:
            ahead[h, 1, part, dc].wait_recv()
    adam(BESIDE_LONG)

    tiles_v[0] = jnp.broadcast_to(by_lane(adam_v[...]), (8, 128))

    def tell(dz):
        return pltpu.make_async_remote_copy(
            src_ref=tiles_v.at[0],
            dst_ref=tiles_v.at[dz],
            send_sem=zsend.at[dz],
            recv_sem=zrecv.at[dz],
            device_id=(me, lax.rem(z + dz, N_Z)),
            device_id_type=MESH,
        )

    for dz in range(1, N_Z):
        tell(dz).start()
    multiply(BESIDE_LONG)
    sum_pre = by_lane(square_v[...])
    for group in (via, straight, onward, far, ahead, inside, passed):
        for copy in group.values():
            copy.wait_send()
    for t in range(4):
        for chunk in range(RING):
            for part in range(2):
                if travels(part, t, chunk):
                    ring_out(part, t, chunk).wait_send()
    for dz in range(1, N_Z):
        tell(dz).wait()
    sum_adam = jnp.sum(tiles_v[...], axis=0)[:1]
    scale = live_v[...] * (jnp.sqrt(sum_adam / total) / jnp.sqrt(sum_pre / total + 1e-06))
    by_row = jnp.where(diagonal, jnp.broadcast_to(scale, (slots, 128)), 0.0)
    scale_out[...] = jnp.broadcast_to(jnp.sum(by_row, axis=1, keepdims=True), (slots, 128))


def step(owner, grads, left, right, mone, mtwo):
    per_shard, order, _ = grads.shape
    slots, share, _ = mone.shape
    block = (order, order)
    anywhere = pl.BlockSpec(memory_space=pl.ANY)
    vmem = pl.BlockSpec(memory_space=pltpu.VMEM)
    dma = pltpu.SemaphoreType.DMA
    return pl.pallas_call(
        step_kernel,
        out_shape=(
            pltpu.VMEM((slots, *block), jnp.bfloat16),
            pltpu.VMEM((slots, 128), jnp.float32),
        ),
        in_specs=[vmem] + [anywhere] * 5,
        out_specs=(vmem, vmem),
        scratch_shapes=[
            pltpu.VMEM((per_shard + 1, *block), jnp.bfloat16),
            pltpu.VMEM((2, 3, 8, *block), jnp.bfloat16),
            pltpu.VMEM((2, 4, 8, *block), jnp.bfloat16),
            pltpu.VMEM((2, 2, 4, *block), jnp.bfloat16),
            pltpu.VMEM((2, 2, 4, *block), jnp.bfloat16),
            pltpu.VMEM((N_Z, slots, share, order), jnp.bfloat16),
            pltpu.VMEM((slots, *block), jnp.bfloat16),
            pltpu.VMEM((slots, share, order), jnp.float32),
            pltpu.VMEM((slots, share, order), jnp.float32),
            pltpu.VMEM((slots, 8, 128), jnp.float32),
            pltpu.VMEM((slots, 8, 128), jnp.float32),
            pltpu.VMEM((N_Z, 8, 128), jnp.float32),
            pltpu.VMEM((1, 128), jnp.float32),
            pltpu.VMEM((1, 128), jnp.int32),
            pltpu.SMEM((1, 128), jnp.int32),
            dma((4,)),
            dma((RING,)),
            dma((2, 2)),
            dma,
            dma((58,)),
            dma((58,)),
            dma((2, 4, RING)),
            dma((2, 4, RING)),
            dma((N_Z,)),
            dma((N_Z,)),
        ],
        compiler_params=pltpu.CompilerParams(
            collective_id=0, has_side_effects=True, vmem_limit_bytes=LIMIT * 2**20
        ),
        cost_estimate=pl.CostEstimate(
            flops=4 * slots * order**3, bytes_accessed=4 * 10**8, transcendentals=10**6
        ),
    )(owner, grads, left, right, mone, mtwo)


def place_of(me, slot):
    y, x, c = me // (N_X * N_C), (me // N_C) % N_X, me % N_C
    source, half = slot // 2, lax.rem(slot, 2)
    dy = lax.rem(source // (N_X * N_C) - y + N_Y, N_Y)
    dx = lax.rem(lax.rem(source // N_C, N_X) - x + N_X, N_X)
    dc = lax.rem(source + c, N_C)
    first, second = dx + half * (dy - dx), dy + half * (dx - dy)
    d = lax.rem(first + 1, 4)
    g, beside = half * 2 + dc, half * 2 + (3 - second) // 2
    near = jnp.where(d == 3, START[NEAR_LONG] + g, START[NEAR] + 3 * g + d)
    away = jnp.where(d == 3, START[AWAY_LONG] + g, START[AWAY] + 3 * g + d)
    cross = START[BESIDE] + dc * (START[BESIDE_CROSS] - START[BESIDE])
    middle = jnp.where(d == 3, START[BESIDE_LONG] + dc * 4 + beside, cross + 3 * beside + d)
    return jnp.where(second == 0, near, jnp.where(second == 2, away, middle))


def scale_kernel(x, scale, out, ready, sems):
    me = lax.axis_index("dp")

    def copy(i):
        some = pl.ds(GROUP * i, GROUP)
        return pltpu.make_async_copy(ready.at[some], out.at[some], sems.at[i])

    def one(i, carry):
        for j in range(GROUP):
            k = GROUP * i + j
            row = scale[pl.ds(k, 1), :]
            factor = jnp.concatenate([row, row], axis=1)
            ready[k] = (x[place_of(me, k)].astype(jnp.float32) * factor).astype(jnp.bfloat16)
        copy(i).start()
        return carry

    def settle(i, carry):
        copy(i).wait()
        return carry

    steps = x.shape[0] // GROUP
    lax.fori_loop(0, steps, one, 0)
    lax.fori_loop(0, steps, settle, 0)


def apply_scale(x, scale):
    vmem = pl.BlockSpec(memory_space=pltpu.VMEM)
    return pl.pallas_call(
        scale_kernel,
        out_shape=jax.ShapeDtypeStruct(x.shape, jnp.bfloat16),
        in_specs=[vmem, vmem],
        out_specs=pl.BlockSpec(memory_space=pl.ANY),
        scratch_shapes=[
            pltpu.VMEM(x.shape, jnp.bfloat16),
            pltpu.SemaphoreType.DMA((x.shape[0] // GROUP,)),
        ],
        compiler_params=pltpu.CompilerParams(vmem_limit_bytes=24 * 2**20),
    )(x, scale)


def per_device(grads, owner, left_root, right_root, first_moment, second_moment):
    x, scale = step(
        owner.reshape(1, -1), grads, left_root[0], right_root[0], first_moment[0], second_moment[0]
    )
    return apply_scale(x, scale)[None]


def solution(mesh):
    placed = (
        P("dp", None, None),
        P(),
        P("dp", None, "replica", None),
        P("dp", None, None, None),
        P("dp", None, "replica", None),
        P("dp", None, "replica", None),
    )
    return jax.shard_map(
        per_device, mesh=mesh, in_specs=placed, out_specs=P("dp", None, None, None), check_vma=False
    )
```

time: 114 us -> 127 us (1.11)
  Pallas kernels: 114 us -> 126 us
    pallas_call x1, Pallas kernels: 108 us -> 122 us  [step(): pl.pallas_call(step_kernel, out_shape=(pltpu.VMEM((slots, *block), jnp.bf...]
    pallas_call x1, Pallas kernels: 5.35 us -> 3.83 us  [apply_scale(): pl.pallas_call(scale_kernel, out_shape=jax.ShapeDtypeStruct(x.shape, jnp....]
where the time goes in v2:
time: 127 us; the launch traced here: 126 us
  Pallas kernels  126 us (99%)
    pallas_call x1, Pallas kernels, step(): pl.pallas_call(step_kernel, out_shape=(pltpu.VMEM((slots, *block), jnp.bf...  122 us
    pallas_call x1, Pallas kernels, apply_scale(): pl.pallas_call(scale_kernel, out_shape=jax.ShapeDtypeStruct(x.shape, jnp....  3.83 us

profile of v2, /device:TPU:1, one launch (start us, length us, event | category | flops | bytes accessed | tf_op | source)
XLA Modules:
  0.0 125.8 jit_solution(6868974117868392820)
XLA Ops:
  0.0 122.0 %shard_map.64 = (bf16[64,256,256]{2,1,0:T(8,128)(2,1)S(1)}, f32[64,128]{1,0:T(8,128)S(1)}) custom-call(s32[1,1024]{1,0:T(1,128)} %bitcast.10, bf16[32,256,256]{2,1,0:T(8,128)(2,1)} %grads_hbm.1, bf16[64,32,256]{2,1,0:T(8,128)(2,1)} %bitcast.9, bf16[64,256,256]{2,1,0:T(8,128)(2,1)} %bitcast.6, f32[64,32,256]{2,1,0:T(8,128)} %bitcast.7, f32[64,32,256]{2,1,0:T(8,128)} %bitcast.8), custom_call_target="tpu_custom_call" | custom-call | flops 4294967296 | bytes 400000000 | tf_op jit(solution)/shard_map/pallas_call | solution.py:405
  122.0 3.8 %shard_map.65 = bf16[64,256,256]{2,1,0:T(8,128)(2,1)} custom-call(bf16[64,256,256]{2,1,0:T(8,128)(2,1)S(1)} %get-tuple-element.7.x, f32[64,128]{1,0:T(8,128)S(1)} %get-tuple-element.8.scale), custom_call_target="tpu_custom_call" | custom-call | tf_op jit(solution)/shard_map/pallas_call | solution.py:492

commit v3 on v2

--- a/solution.py
+++ b/solution.py
@@ -205,37 +205,38 @@
         values = values[:, :128] + values[:, 128:]
         return jnp.sum(values.reshape(values.shape[0] // 8, 8, 128), axis=0)
 
-    def adam(kind):
-        def some(i, carry):
-            for j in range(4):
-                pos = START[kind] + 4 * i + j
-                k = slot_of(kind, pos)
+    def in_fours(kind, some):
+        def one(i, carry):
+            places = [START[kind] + 4 * i + j for j in range(4)]
+            some(places, [slot_of(kind, pos) for pos in places])
+            return carry
+
+        lax.fori_loop(0, (START[kind + 1] - START[kind]) // 4, one, 0)
+
+    def absorb(kind):
+        def some(places, ks):
+            for pos, k in zip(places, ks):
                 grad32 = recv_v[pos, rows, :].astype(jnp.float32)
                 moment_one = 0.9 * mone_v[k] + 0.1 * grad32
                 moment_two = 0.999 * mtwo_v[k] + 0.001 * grad32 * grad32
                 ratio = moment_one / (jnp.sqrt(moment_two) + 1e-08)
                 adam_v[k] = fold(ratio * ratio)
-            return carry
-
-        lax.fori_loop(0, (START[kind + 1] - START[kind]) // 4, some, 0)
-
-    def multiply(kind):
-        def some(i, carry):
-            places = [START[kind] + 4 * i + j for j in range(4)]
-            ks = [slot_of(kind, pos) for pos in places]
-            halves = [
-                jnp.dot(
+            for pos, k in zip(places, ks):
+                product = jnp.dot(recv_v[pos], right_v[k], preferred_element_type=jnp.float32)
+                recv_v[pos] = product.astype(jnp.bfloat16)
+
+        in_fours(kind, some)
+
+    def finish(kind):
+        def some(places, ks):
+            for pos, k in zip(places, ks):
+                precond = jnp.dot(
                     left_v[:, pos].reshape(order, order), recv_v[pos], preferred_element_type=jnp.float32
-                ).astype(jnp.bfloat16)
-                for pos in places
-            ]
-            for pos, k, half in zip(places, ks, halves):
-                precond = jnp.dot(half, right_v[k], preferred_element_type=jnp.float32)
+                )
                 square_v[k] = fold(precond * precond)
                 recv_v[pos] = precond.astype(jnp.bfloat16)
-            return carry
-
-        lax.fori_loop(0, (START[kind + 1] - START[kind]) // 4, some, 0)
+
+        in_fours(kind, some)
 
     def count_live():
         shard = lax.broadcasted_iota(jnp.int32, (owner.shape[1], 128), 0) // per_shard
@@ -268,8 +269,7 @@
     for chunk in range(RING):
         first = pl.ds(chunk * per_ring, per_ring)
         pltpu.make_async_copy(left_hbm.at[first], left_v.at[z, first], left_sems.at[chunk]).wait()
-        if chunk < 2:
-            begin(chunk)
+        begin(chunk)
     for h, part in every:
         pack(h, SIGNS[part], range(8), out_v.at[h, part])
         straight[h, part].start()
@@ -279,89 +279,73 @@
     for h in range(2):
         pack(h, 0, range(8), stage_v.at[h, 1])
 
-    pass_on(0, 0)
+    for h, part in every:
+        via[h, 0, part].wait_recv()
+        onward[h, 0, part].start()
     for h, part in every:
         onward[h, 1, part].wait_recv()
         far[h, 1, part].start()
-    pass_on(0, 1)
-    for h, part in every:
-        via[h, 0, part].wait_recv()
-        onward[h, 0, part].start()
+    count_live()
+    pass_on(0, 0, 1, 2, 3)
     for h, part in every:
         far[h, 1, part].wait_recv()
         passed[h, 1, part].start()
-    pass_on(1, 0)
+    for h, part in every:
+        straight[h, part].wait_recv()
+    for h, part in every:
+        far[h, 0, part].start()
+    for h, part in every:
+        ahead[h, 0, part, 0].start()
+    for h in range(2):
+        inside[h, 0].start()
+        own[h, 0].start()
     for h in range(2):
         for part in range(2):
             passed[h, 1, part].wait_recv()
         swap[h].start()
-    pass_on(1, 1)
-    begin(2)
-    for load in loads[1:]:
-        load.wait()
-    count_live()
-    pass_on(2, 0)
-    for h, part in every:
-        straight[h, part].wait_recv()
-    for h, part in every:
-        far[h, 0, part].start()
-    for h in range(2):
-        inside[h, 0].start()
-        own[h, 0].start()
-    pass_on(2, 1)
-    begin(3)
-    for h, part in every:
-        ahead[h, 0, part, 0].start()
-    for h in range(2):
-        swapped[h].wait_recv()
-        swap[h].wait_send()
-    adam(AWAY_LONG)
-    pass_on(0, 2)
+    pass_on(1, 0, 1, 2, 3)
     for h, part in every:
         onward[h, 0, part].wait_recv()
     for h in range(2):
         inside[h, 1].start()
         own[h, 1].start()
-    pass_on(3, 0, 1)
-    multiply(AWAY_LONG)
-    pass_on(0, 3)
+    for load in loads[1:]:
+        load.wait()
     for m in range(2):
         for h in range(2):
             own[h, m].wait()
             inside[h, m].wait_recv()
-        adam((NEAR, NEAR_LONG)[m])
+    absorb(NEAR)
     for h, part in every:
         far[h, 0, part].wait_recv()
         passed[h, 0, part].start()
-    multiply(NEAR)
-    pass_on(1, 2)
-    multiply(NEAR_LONG)
     for h, part in every:
         ahead[h, 0, part, 0].wait_recv()
     for h, part in every:
         ahead[h, 0, part, 1].start()
-    pass_on(1, 3)
-    adam(BESIDE)
-    multiply(BESIDE)
-    pass_on(2, 2)
+    for h in range(2):
+        swapped[h].wait_recv()
+        swap[h].wait_send()
+    absorb(NEAR_LONG)
+    absorb(AWAY_LONG)
+    absorb(BESIDE)
+    pass_on(2, 0, 1, 2, 3)
     for h, part in every:
         passed[h, 0, part].wait_recv()
     for dc in range(N_C):
         for h, part in every:
             ahead[h, 1, part, dc].start()
-    adam(AWAY)
-    pass_on(2, 3)
-    pass_on(3, 2)
-    multiply(AWAY)
+    absorb(AWAY)
     for h, part in every:
         ahead[h, 0, part, 1].wait_recv()
-    adam(BESIDE_CROSS)
-    pass_on(3, 3)
-    multiply(BESIDE_CROSS)
+    absorb(BESIDE_CROSS)
+    pass_on(3, 0, 1)
+    for kind in (NEAR, NEAR_LONG, BESIDE, AWAY_LONG):
+        finish(kind)
     for dc in range(N_C):
         for h, part in every:
             ahead[h, 1, part, dc].wait_recv()
-    adam(BESIDE_LONG)
+    absorb(BESIDE_LONG)
 
     tiles_v[0] = jnp.broadcast_to(by_lane(adam_v[...]), (8, 128))
 
@@ -377,7 +361,9 @@
 
     for dz in range(1, N_Z):
         tell(dz).start()
-    multiply(BESIDE_LONG)
+    pass_on(3, 2, 3)
+    for kind in (AWAY, BESIDE_CROSS, BESIDE_LONG):
+        finish(kind)
     sum_pre = by_lane(square_v[...])
     for group in (via, straight, onward, far, ahead, inside, passed):
         for copy in group.values():

time: 127 us -> 117 us (0.921)
  Pallas kernels: 126 us -> 116 us
    pallas_call x1, Pallas kernels: 122 us -> 112 us  [step(): pl.pallas_call(step_kernel, out_shape=(pltpu.VMEM((slots, *block), jnp.bf...]
where the time goes in v3:
time: 117 us; the launch traced here: 116 us
  Pallas kernels  116 us (99%)
    pallas_call x1, Pallas kernels, step(): pl.pallas_call(step_kernel, out_shape=(pltpu.VMEM((slots, *block), jnp.bf...  112 us
    pallas_call x1, Pallas kernels, apply_scale(): pl.pallas_call(scale_kernel, out_shape=jax.ShapeDtypeStruct(x.shape, jnp....  3.83 us

profile of v3, /device:TPU:1, one launch (start us, length us, event | category | flops | bytes accessed | tf_op | source)
XLA Modules:
  0.0 116.1 jit_solution(4488724612428671764)
XLA Ops:
  0.0 112.2 %shard_map.64 = (bf16[64,256,256]{2,1,0:T(8,128)(2,1)S(1)}, f32[64,128]{1,0:T(8,128)S(1)}) custom-call(s32[1,1024]{1,0:T(1,128)} %bitcast.10, bf16[32,256,256]{2,1,0:T(8,128)(2,1)} %grads_hbm.1, bf16[64,32,256]{2,1,0:T(8,128)(2,1)} %bitcast.9, bf16[64,256,256]{2,1,0:T(8,128)(2,1)} %bitcast.6, f32[64,32,256]{2,1,0:T(8,128)} %bitcast.7, f32[64,32,256]{2,1,0:T(8,128)} %bitcast.8), custom_call_target="tpu_custom_call" | custom-call | flops 4294967296 | bytes 400000000 | tf_op jit(solution)/shard_map/pallas_call | solution.py:391
  112.2 3.8 %shard_map.65 = bf16[64,256,256]{2,1,0:T(8,128)(2,1)} custom-call(bf16[64,256,256]{2,1,0:T(8,128)(2,1)S(1)} %get-tuple-element.7.x, f32[64,128]{1,0:T(8,128)S(1)} %get-tuple-element.8.scale), custom_call_target="tpu_custom_call" | custom-call | tf_op jit(solution)/shard_map/pallas_call | solution.py:478

commit v4 on v3

--- a/solution.py
+++ b/solution.py
@@ -129,7 +129,8 @@
     for h in range(2):
         for part, sign in enumerate(SIGNS):
             there = along(h, sign, 0, 0)
-            straight[h, part] = message(out_v.at[h, part], stage_v.at[h, 2 * part], there)
+            for b, some in enumerate((*FULL, pl.ds(3, 2))):
+                straight[h, b, part] = message(out_v.at[h, part, some], stage_v.at[h, 2 * part, some], there)
             via[h, 0, part] = message(out_v.at[h, 2, FULL[part]], pass_v.at[h, part, pl.ds(0, 3)], there)
             onward[h, 0, part] = message(pass_v.at[h, part, pl.ds(0, 3)], stage_v.at[h, 3, FULL[part]], there)
             via[h, 1, part] = message(
@@ -260,50 +261,71 @@
     )
 
     every = [(h, part) for h in range(2) for part in range(2)]
-    for h, part in every:
-        pack(h, 2, (3 + part,), out_v.at[h, 2])
-        via[h, 1, part].start()
-    for h, part in every:
-        pack(h, 2, ((0, 1, 2), (5, 6, 7))[part], out_v.at[h, 2])
-        via[h, 0, part].start()
-    for chunk in range(RING):
+    thirds = ((0, 1, 2), (5, 6, 7), (3, 4))
+
+    def ready(chunk):
         first = pl.ds(chunk * per_ring, per_ring)
         pltpu.make_async_copy(left_hbm.at[first], left_v.at[z, first], left_sems.at[chunk]).wait()
         begin(chunk)
-    for h, part in every:
-        pack(h, SIGNS[part], range(8), out_v.at[h, part])
-        straight[h, part].start()
+
+    for h, part in every:
+        pack(h, 2, (3 + part,), out_v.at[h, 2])
+        via[h, 1, part].start()
+    for h, part in every:
+        pack(h, SIGNS[part], thirds[2], out_v.at[h, part])
+        straight[h, 2, part].start()
+    for h, part in every:
+        pack(h, 2, thirds[part], out_v.at[h, 2])
+        via[h, 0, part].start()
+    ready(0)
+    ready(1)
+    for h in range(2):
+        pack(h, 0, thirds[2], stage_v.at[h, 1])
     for h, part in every:
         via[h, 1, part].wait_recv()
         onward[h, 1, part].start()
-    for h in range(2):
-        pack(h, 0, range(8), stage_v.at[h, 1])
-
+    for h, part in every:
+        for b in range(2):
+            pack(h, SIGNS[part], thirds[b], out_v.at[h, part])
+            straight[h, b, part].start()
+    ready(2)
+    ready(3)
+    for h in range(2):
+        for b in range(2):
+            pack(h, 0, thirds[b], stage_v.at[h, 1])
+    count_live()
+
+    for h, part in every:
+        straight[h, 2, part].wait_recv()
+    for h, part in every:
+        far[h, 0, part].start()
+    for h, part in every:
+        onward[h, 1, part].wait_recv()
+        far[h, 1, part].start()
     for h, part in every:
         via[h, 0, part].wait_recv()
         onward[h, 0, part].start()
-    for h, part in every:
-        onward[h, 1, part].wait_recv()
-        far[h, 1, part].start()
-    count_live()
-    pass_on(0, 0, 1, 2, 3)
+    pass_on(0, 0, 1)
     for h, part in every:
         far[h, 1, part].wait_recv()
         passed[h, 1, part].start()
-    for h, part in every:
-        straight[h, part].wait_recv()
-    for h, part in every:
-        far[h, 0, part].start()
-    for h, part in every:
-        ahead[h, 0, part, 0].start()
-    for h in range(2):
-        inside[h, 0].start()
-        own[h, 0].start()
+    pass_on(0, 2, 3)
     for h in range(2):
         for part in range(2):
             passed[h, 1, part].wait_recv()
         swap[h].start()
-    pass_on(1, 0, 1, 2, 3)
+    for h, part in every:
+        far[h, 0, part].wait_recv()
+        passed[h, 0, part].start()
+    for h, part in every:
+        for b in range(2):
+            straight[h, b, part].wait_recv()
+    for h, part in every:
+        ahead[h, 0, part, 0].start()
+    for h in range(2):
+        inside[h, 0].start()
+        own[h, 0].start()
+    pass_on(1, 0, 1)
     for h, part in every:
         onward[h, 0, part].wait_recv()
     for h in range(2):
@@ -317,31 +339,27 @@
             inside[h, m].wait_recv()
     absorb(NEAR)
     for h, part in every:
-        far[h, 0, part].wait_recv()
-        passed[h, 0, part].start()
-    for h, part in every:
-        ahead[h, 0, part, 0].wait_recv()
-    for h, part in every:
         ahead[h, 0, part, 1].start()
+    pass_on(1, 2, 3)
+    absorb(NEAR_LONG)
     for h in range(2):
         swapped[h].wait_recv()
         swap[h].wait_send()
-    absorb(NEAR_LONG)
     absorb(AWAY_LONG)
-    absorb(BESIDE)
-    pass_on(2, 0, 1, 2, 3)
-    for h, part in every:
-        passed[h, 0, part].wait_recv()
+    for h, part in every:
+        ahead[h, 0, part, 0].wait_recv()
     for dc in range(N_C):
         for h, part in every:
             ahead[h, 1, part, dc].start()
+    absorb(BESIDE)
+    pass_on(2, 0, 1)
+    for h, part in every:
+        passed[h, 0, part].wait_recv()
     absorb(AWAY)
+    pass_on(2, 2, 3)
     for h, part in every:
         ahead[h, 0, part, 1].wait_recv()
     absorb(BESIDE_CROSS)
-    pass_on(3, 0, 1)
-    for kind in (NEAR, NEAR_LONG, BESIDE, AWAY_LONG):
-        finish(kind)
     for dc in range(N_C):
         for h, part in every:
             ahead[h, 1, part, dc].wait_recv()
@@ -361,8 +379,13 @@
 
     for dz in range(1, N_Z):
         tell(dz).start()
-    pass_on(3, 2, 3)
-    for kind in (AWAY, BESIDE_CROSS, BESIDE_LONG):
+    pass_on(3, 0, 1)
+    for kind in (NEAR, NEAR_LONG, BESIDE, AWAY_LONG):
+        finish(kind)
+    pass_on(3, 2)
+    finish(AWAY)
+    pass_on(3, 3)
+    for kind in (BESIDE_CROSS, BESIDE_LONG):
         finish(kind)
     sum_pre = by_lane(square_v[...])
     for group in (via, straight, onward, far, ahead, inside, passed):
@@ -416,8 +439,8 @@
             dma((RING,)),
             dma((2, 2)),
             dma,
-            dma((58,)),
-            dma((58,)),
+            dma((66,)),
+            dma((66,)),
             dma((2, 4, RING)),
             dma((2, 4, RING)),
             dma((N_Z,)),

time: 117 us -> 114 us (0.974)
  Pallas kernels: 116 us -> 114 us
    pallas_call x1, Pallas kernels: 112 us -> 110 us  [step(): pl.pallas_call(step_kernel, out_shape=(pltpu.VMEM((slots, *block), jnp.bf...]
where the time goes in v4:
time: 114 us
  Pallas kernels  114 us (100%)
    pallas_call x1, Pallas kernels, step(): pl.pallas_call(step_kernel, out_shape=(pltpu.VMEM((slots, *block), jnp.bf...  110 us
    pallas_call x1, Pallas kernels, apply_scale(): pl.pallas_call(scale_kernel, out_shape=jax.ShapeDtypeStruct(x.shape, jnp....  3.83 us

profile of v4, /device:TPU:1, one launch (start us, length us, event | category | flops | bytes accessed | tf_op | source)
XLA Modules:
  0.0 113.6 jit_solution(15981654116548586525)
XLA Ops:
  0.0 109.8 %shard_map.64 = (bf16[64,256,256]{2,1,0:T(8,128)(2,1)S(1)}, f32[64,128]{1,0:T(8,128)S(1)}) custom-call(s32[1,1024]{1,0:T(1,128)} %bitcast.10, bf16[32,256,256]{2,1,0:T(8,128)(2,1)} %grads_hbm.1, bf16[64,32,256]{2,1,0:T(8,128)(2,1)} %bitcast.9, bf16[64,256,256]{2,1,0:T(8,128)(2,1)} %bitcast.6, f32[64,32,256]{2,1,0:T(8,128)} %bitcast.7, f32[64,32,256]{2,1,0:T(8,128)} %bitcast.8), custom_call_target="tpu_custom_call" | custom-call | flops 4294967296 | bytes 400000000 | tf_op jit(solution)/shard_map/pallas_call | solution.py:414
  109.8 3.8 %shard_map.65 = bf16[64,256,256]{2,1,0:T(8,128)(2,1)} custom-call(bf16[64,256,256]{2,1,0:T(8,128)(2,1)S(1)} %get-tuple-element.7.x, f32[64,128]{1,0:T(8,128)S(1)} %get-tuple-element.8.scale), custom_call_target="tpu_custom_call" | custom-call | tf_op jit(solution)/shard_map/pallas_call | solution.py:501

commit v5 on v3

--- a/solution.py
+++ b/solution.py
@@ -129,7 +129,8 @@
     for h in range(2):
         for part, sign in enumerate(SIGNS):
             there = along(h, sign, 0, 0)
-            straight[h, part] = message(out_v.at[h, part], stage_v.at[h, 2 * part], there)
+            for b, some in enumerate((*FULL, pl.ds(3, 2))):
+                straight[h, b, part] = message(out_v.at[h, part, some], stage_v.at[h, 2 * part, some], there)
             via[h, 0, part] = message(out_v.at[h, 2, FULL[part]], pass_v.at[h, part, pl.ds(0, 3)], there)
             onward[h, 0, part] = message(pass_v.at[h, part, pl.ds(0, 3)], stage_v.at[h, 3, FULL[part]], there)
             via[h, 1, part] = message(
@@ -205,15 +206,18 @@
         values = values[:, :128] + values[:, 128:]
         return jnp.sum(values.reshape(values.shape[0] // 8, 8, 128), axis=0)
 
-    def in_fours(kind, some):
+    def in_fours(kind, some, only=None):
         def one(i, carry):
             places = [START[kind] + 4 * i + j for j in range(4)]
             some(places, [slot_of(kind, pos) for pos in places])
             return carry
 
-        lax.fori_loop(0, (START[kind + 1] - START[kind]) // 4, one, 0)
-
-    def absorb(kind):
+        if only is None:
+            lax.fori_loop(0, (START[kind + 1] - START[kind]) // 4, one, 0)
+        else:
+            one(only, 0)
+
+    def absorb(kind, only=None):
         def some(places, ks):
             for pos, k in zip(places, ks):
                 grad32 = recv_v[pos, rows, :].astype(jnp.float32)
@@ -225,7 +229,7 @@
                 product = jnp.dot(recv_v[pos], right_v[k], preferred_element_type=jnp.float32)
                 recv_v[pos] = product.astype(jnp.bfloat16)
 
-        in_fours(kind, some)
+        in_fours(kind, some, only)
 
     def finish(kind):
         def some(places, ks):
@@ -260,55 +264,66 @@
     )
 
     every = [(h, part) for h in range(2) for part in range(2)]
-    for h, part in every:
-        pack(h, 2, (3 + part,), out_v.at[h, 2])
-        via[h, 1, part].start()
-    for h, part in every:
-        pack(h, 2, ((0, 1, 2), (5, 6, 7))[part], out_v.at[h, 2])
-        via[h, 0, part].start()
-    for chunk in range(RING):
+    thirds = ((0, 1, 2), (5, 6, 7), (3, 4))
+
+    def ready(chunk):
         first = pl.ds(chunk * per_ring, per_ring)
         pltpu.make_async_copy(left_hbm.at[first], left_v.at[z, first], left_sems.at[chunk]).wait()
         begin(chunk)
-    for h, part in every:
-        pack(h, SIGNS[part], range(8), out_v.at[h, part])
-        straight[h, part].start()
+
+    for chunk in range(RING):
+        ready(chunk)
+    for h, part in every:
+        pack(h, 2, (3 + part,), out_v.at[h, 2])
+        via[h, 1, part].start()
+    for h, part in every:
+        pack(h, 2, thirds[part], out_v.at[h, 2])
+        via[h, 0, part].start()
+    for h, part in every:
+        pack(h, SIGNS[part], thirds[2], out_v.at[h, part])
+        straight[h, 2, part].start()
     for h, part in every:
         via[h, 1, part].wait_recv()
         onward[h, 1, part].start()
+    for b in range(2):
+        for h, part in every:
+            pack(h, SIGNS[part], thirds[b], out_v.at[h, part])
+            straight[h, b, part].start()
     for h in range(2):
         pack(h, 0, range(8), stage_v.at[h, 1])
-
+    count_live()
+
+    pass_on(0, 0)
     for h, part in every:
         via[h, 0, part].wait_recv()
         onward[h, 0, part].start()
+    pass_on(0, 1)
     for h, part in every:
         onward[h, 1, part].wait_recv()
         far[h, 1, part].start()
-    count_live()
-    pass_on(0, 0, 1, 2, 3)
-    for h, part in every:
-        far[h, 1, part].wait_recv()
-        passed[h, 1, part].start()
-    for h, part in every:
-        straight[h, part].wait_recv()
+    for h, part in every:
+        straight[h, 2, part].wait_recv()
     for h, part in every:
         far[h, 0, part].start()
+    pass_on(0, 2, 3)
+    pass_on(1, 0)
+    for h, part in every:
+        for b in range(2):
+            straight[h, b, part].wait_recv()
     for h, part in every:
         ahead[h, 0, part, 0].start()
     for h in range(2):
         inside[h, 0].start()
         own[h, 0].start()
-    for h in range(2):
-        for part in range(2):
-            passed[h, 1, part].wait_recv()
-        swap[h].start()
-    pass_on(1, 0, 1, 2, 3)
+    pass_on(1, 1, 2)
     for h, part in every:
         onward[h, 0, part].wait_recv()
     for h in range(2):
         inside[h, 1].start()
         own[h, 1].start()
+    for h, part in every:
+        far[h, 1, part].wait_recv()
+        passed[h, 1, part].start()
     for load in loads[1:]:
         load.wait()
     for m in range(2):
@@ -316,36 +331,46 @@
             own[h, m].wait()
             inside[h, m].wait_recv()
     absorb(NEAR)
+    absorb(NEAR_LONG)
+    pass_on(1, 3)
     for h, part in every:
         far[h, 0, part].wait_recv()
         passed[h, 0, part].start()
     for h, part in every:
+        ahead[h, 0, part, 1].start()
+    for dc in range(N_C):
+        for h, part in every:
+            ahead[h, 1, part, dc].start()
+    pass_on(2, 0, 1)
+    for h, part in every:
         ahead[h, 0, part, 0].wait_recv()
-    for h, part in every:
-        ahead[h, 0, part, 1].start()
+    for h in range(2):
+        for part in range(2):
+            passed[h, 1, part].wait_recv()
+        swap[h].start()
+    absorb(BESIDE)
+    pass_on(2, 2, 3)
+    for h, part in every:
+        passed[h, 0, part].wait_recv()
+    absorb(AWAY)
+    pass_on(3, 0, 1)
+    for kind in (NEAR, NEAR_LONG, BESIDE):
+        finish(kind)
     for h in range(2):
         swapped[h].wait_recv()
         swap[h].wait_send()
-    absorb(NEAR_LONG)
     absorb(AWAY_LONG)
-    absorb(BESIDE)
-    pass_on(2, 0, 1, 2, 3)
-    for h, part in every:
-        passed[h, 0, part].wait_recv()
-    for dc in range(N_C):
-        for h, part in every:
-            ahead[h, 1, part, dc].start()
-    absorb(AWAY)
+    finish(AWAY_LONG)
     for h, part in every:
         ahead[h, 0, part, 1].wait_recv()
     absorb(BESIDE_CROSS)
-    pass_on(3, 0, 1)
-    for kind in (NEAR, NEAR_LONG, BESIDE, AWAY_LONG):
-        finish(kind)
+    pass_on(3, 2)
+    finish(AWAY)
+    pass_on(3, 3)
     for dc in range(N_C):
         for h, part in every:
             ahead[h, 1, part, dc].wait_recv()
-    absorb(BESIDE_LONG)
+        absorb(BESIDE_LONG, dc)
 
     tiles_v[0] = jnp.broadcast_to(by_lane(adam_v[...]), (8, 128))
 
@@ -361,9 +386,8 @@
 
     for dz in range(1, N_Z):
         tell(dz).start()
-    pass_on(3, 2, 3)
-    for kind in (AWAY, BESIDE_CROSS, BESIDE_LONG):
-        finish(kind)
+    finish(BESIDE_CROSS)
+    finish(BESIDE_LONG)
     sum_pre = by_lane(square_v[...])
     for group in (via, straight, onward, far, ahead, inside, passed):
         for copy in group.values():
@@ -416,8 +440,8 @@
             dma((RING,)),
             dma((2, 2)),
             dma,
-            dma((58,)),
-            dma((58,)),
+            dma((66,)),
+            dma((66,)),
             dma((2, 4, RING)),
             dma((2, 4, RING)),
             dma((N_Z,)),

time: 117 us -> 107 us (0.915)
  Pallas kernels: 116 us -> 107 us
    pallas_call x1, Pallas kernels: 112 us -> 103 us  [step(): pl.pallas_call(step_kernel, out_shape=(pltpu.VMEM((slots, *block), jnp.bf...]
where the time goes in v5:
time: 107 us
  Pallas kernels  107 us (100%)
    pallas_call x1, Pallas kernels, step(): pl.pallas_call(step_kernel, out_shape=(pltpu.VMEM((slots, *block), jnp.bf...  103 us
    pallas_call x1, Pallas kernels, apply_scale(): pl.pallas_call(scale_kernel, out_shape=jax.ShapeDtypeStruct(x.shape, jnp....  3.83 us

profile of v5, /device:TPU:1, one launch (start us, length us, event | category | flops | bytes accessed | tf_op | source)
XLA Modules:
  0.0 107.0 jit_solution(14777238696869434798)
XLA Ops:
  0.0 103.1 %shard_map.64 = (bf16[64,256,256]{2,1,0:T(8,128)(2,1)S(1)}, f32[64,128]{1,0:T(8,128)S(1)}) custom-call(s32[1,1024]{1,0:T(1,128)} %bitcast.10, bf16[32,256,256]{2,1,0:T(8,128)(2,1)} %grads_hbm.1, bf16[64,32,256]{2,1,0:T(8,128)(2,1)} %bitcast.9, bf16[64,256,256]{2,1,0:T(8,128)(2,1)} %bitcast.6, f32[64,32,256]{2,1,0:T(8,128)} %bitcast.7, f32[64,32,256]{2,1,0:T(8,128)} %bitcast.8), custom_call_target="tpu_custom_call" | custom-call | flops 4294967296 | bytes 400000000 | tf_op jit(solution)/shard_map/pallas_call | solution.py:415
  103.1 3.8 %shard_map.65 = bf16[64,256,256]{2,1,0:T(8,128)(2,1)} custom-call(bf16[64,256,256]{2,1,0:T(8,128)(2,1)S(1)} %get-tuple-element.7.x, f32[64,128]{1,0:T(8,128)S(1)} %get-tuple-element.8.scale), custom_call_target="tpu_custom_call" | custom-call | tf_op jit(solution)/shard_map/pallas_call | solution.py:502

commit v6 on v5

--- a/solution.py
+++ b/solution.py
@@ -36,7 +36,7 @@
 def step_kernel(
     owner, grads_hbm, left_hbm, right_hbm, mone_hbm, mtwo_hbm, recv_v, scale_out,
     grads_v, out_v, stage_v, pass_v, relay_v, left_v, right_v, mone_v, mtwo_v,
-    adam_v, square_v, tiles_v, live_v, idx_v, idx,
+    adam_v, square_v, tiles_v, strip_v, live_v, idx_v, idx,
     load_sems, left_sems, own_sems, idx_sem, send_sems, recv_sems, ring_send, ring_recv, zsend, zrecv,
 ):
     me, z = lax.axis_index("dp"), lax.axis_index("replica")
@@ -58,6 +58,19 @@
         half, first, second, dc = decode(kind, pos - START[kind])
         return 2 * along(half, first, second, dc) + half
 
+    quarter = per_shard // 4
+    grad_loads = [
+        pltpu.make_async_copy(grads_hbm.at[some], grads_v.at[some], load_sems.at[i])
+        for i, some in enumerate(pl.ds(quarter * i, quarter) for i in range(4))
+    ]
+    loads = [
+        pltpu.make_async_copy(mone_hbm, mone_v, load_sems.at[4]),
+        pltpu.make_async_copy(mtwo_hbm, mtwo_v, load_sems.at[5]),
+        pltpu.make_async_copy(right_hbm, right_v, load_sems.at[6]),
+    ]
+    for load in grad_loads:
+        load.start()
+
     barrier = pltpu.get_barrier_semaphore()
     near = [(0, 0, 1)] + [(dy, dx, dc) for dy, dx in ((0, 1), (0, -1), (1, 0), (-1, 0)) for dc in range(N_C)]
     for step in near:
@@ -65,13 +78,6 @@
     for dz in range(1, N_Z):
         pl.semaphore_signal(barrier, inc=1, device_id=(me, lax.rem(z + dz, N_Z)), device_id_type=MESH)
 
-    loads = [
-        pltpu.make_async_copy(grads_hbm, grads_v.at[pl.ds(0, per_shard)], load_sems.at[0]),
-        pltpu.make_async_copy(mone_hbm, mone_v, load_sems.at[1]),
-        pltpu.make_async_copy(mtwo_hbm, mtwo_v, load_sems.at[2]),
-        pltpu.make_async_copy(right_hbm, right_v, load_sems.at[3]),
-    ]
-    loads[0].start()
     row = lax.broadcasted_iota(jnp.int32, (per_shard, 128), 0)
     lane = lax.broadcasted_iota(jnp.int32, (per_shard, 128), 1)
     per_line = 128 // per_shard
@@ -94,11 +100,7 @@
             return carry
 
         lax.fori_loop(START[kind], START[kind + 1], load_left, 0)
-    for load in loads[1:]:
-        load.start()
     grads_v[per_shard] = jnp.zeros((order, order), jnp.bfloat16)
-    to_scalars.wait()
-    loads[0].wait()
     pl.semaphore_wait(barrier, len(near) + N_Z - 1)
 
     def pack(half, first, places, into):
@@ -125,7 +127,8 @@
     other_rows = pl.ds(pl.multiple_of((1 - parity) * (order // 2), order // 2), order // 2)
     pieces = (pl.ds(0, 3), pl.ds(3, 1))
     via, straight, onward = {}, {}, {}
-    far, ahead, inside, passed, own, swap, swapped = {}, {}, {}, {}, {}, {}, {}
+    far, ahead, inside, passed, own, swap, swapped, strip = {}, {}, {}, {}, {}, {}, {}, {}
+    rows = pl.ds(pl.multiple_of(z * share, share), share)
     for h in range(2):
         for part, sign in enumerate(SIGNS):
             there = along(h, sign, 0, 0)
@@ -151,6 +154,12 @@
             passed[h, 1, part] = message(
                 relay_v.at[h, part, 3, half_rows], recv_v.at[START[AWAY_LONG] + h * 2 + part, half_rows], last
             )
+            for dc in range(N_C):
+                strip[h, part, dc] = message(
+                    stage_v.at[h, 3, PACKED.index((sign % 4, dc)), rows],
+                    strip_v.at[dc * 4 + h * 2 + part],
+                    along(h, 0, sign, dc),
+                )
             for m, piece in enumerate(pieces):
                 for dc in range(N_C):
                     ahead[h, m, part, dc] = message(
@@ -200,8 +209,6 @@
         for part in range(2):
             ring_out(part, 0, chunk).start()
 
-    rows = pl.ds(pl.multiple_of(z * share, share), share)
-
     def fold(values):
         values = values[:, :128] + values[:, 128:]
         return jnp.sum(values.reshape(values.shape[0] // 8, 8, 128), axis=0)
@@ -217,21 +224,32 @@
         else:
             one(only, 0)
 
+    def square_ratio(grad, k):
+        grad32 = grad.astype(jnp.float32)
+        moment_one = 0.9 * mone_v[k] + 0.1 * grad32
+        moment_two = 0.999 * mtwo_v[k] + 0.001 * grad32 * grad32
+        ratio = moment_one / (jnp.sqrt(moment_two) + 1e-08)
+        adam_v[k] = fold(ratio * ratio)
+
     def absorb(kind, only=None):
         def some(places, ks):
-            for pos, k in zip(places, ks):
-                grad32 = recv_v[pos, rows, :].astype(jnp.float32)
-                moment_one = 0.9 * mone_v[k] + 0.1 * grad32
-                moment_two = 0.999 * mtwo_v[k] + 0.001 * grad32 * grad32
-                ratio = moment_one / (jnp.sqrt(moment_two) + 1e-08)
-                adam_v[k] = fold(ratio * ratio)
+            if kind != BESIDE_LONG:
+                for pos, k in zip(places, ks):
+                    square_ratio(recv_v[pos, rows, :], k)
             for pos, k in zip(places, ks):
                 product = jnp.dot(recv_v[pos], right_v[k], preferred_element_type=jnp.float32)
                 recv_v[pos] = product.astype(jnp.bfloat16)
 
         in_fours(kind, some, only)
 
-    def finish(kind):
+    def adam_of_strips():
+        def some(places, ks):
+            for pos, k in zip(places, ks):
+                square_ratio(strip_v[pos - START[BESIDE_LONG]], k)
+
+        in_fours(BESIDE_LONG, some)
+
+    def finish(kind, only=None):
         def some(places, ks):
             for pos, k in zip(places, ks):
                 precond = jnp.dot(
@@ -240,7 +258,7 @@
                 square_v[k] = fold(precond * precond)
                 recv_v[pos] = precond.astype(jnp.bfloat16)
 
-        in_fours(kind, some)
+        in_fours(kind, some, only)
 
     def count_live():
         shard = lax.broadcasted_iota(jnp.int32, (owner.shape[1], 128), 0) // per_shard
@@ -273,6 +291,11 @@
 
     for chunk in range(RING):
         ready(chunk)
+    to_scalars.wait()
+    for load in grad_loads:
+        load.wait()
+    for load in loads:
+        load.start()
     for h, part in every:
         pack(h, 2, (3 + part,), out_v.at[h, 2])
         via[h, 1, part].start()
@@ -324,7 +347,7 @@
     for h, part in every:
         far[h, 1, part].wait_recv()
         passed[h, 1, part].start()
-    for load in loads[1:]:
+    for load in loads:
         load.wait()
     for m in range(2):
         for h in range(2):
@@ -338,6 +361,9 @@
         passed[h, 0, part].start()
     for h, part in every:
         ahead[h, 0, part, 1].start()
+    for dc in range(N_C):
+        for h, part in every:
+            strip[h, part, dc].start()
     for dc in range(N_C):
         for h, part in every:
             ahead[h, 1, part, dc].start()
@@ -364,13 +390,10 @@
     for h, part in every:
         ahead[h, 0, part, 1].wait_recv()
     absorb(BESIDE_CROSS)
-    pass_on(3, 2)
-    finish(AWAY)
-    pass_on(3, 3)
     for dc in range(N_C):
         for h, part in every:
-            ahead[h, 1, part, dc].wait_recv()
-        absorb(BESIDE_LONG, dc)
+            strip[h, part, dc].wait_recv()
+    adam_of_strips()
 
     tiles_v[0] = jnp.broadcast_to(by_lane(adam_v[...]), (8, 128))
 
@@ -386,10 +409,17 @@
 
     for dz in range(1, N_Z):
         tell(dz).start()
+    pass_on(3, 2)
+    finish(AWAY)
+    pass_on(3, 3)
     finish(BESIDE_CROSS)
-    finish(BESIDE_LONG)
+    for dc in range(N_C):
+        for h, part in every:
+            ahead[h, 1, part, dc].wait_recv()
+        absorb(BESIDE_LONG, dc)
+        finish(BESIDE_LONG, dc)
     sum_pre = by_lane(square_v[...])
-    for group in (via, straight, onward, far, ahead, inside, passed):
+    for group in (via, straight, onward, far, ahead, inside, passed, strip):
         for copy in group.values():
             copy.wait_send()
     for t in range(4):
@@ -433,15 +463,16 @@
             pltpu.VMEM((slots, 8, 128), jnp.float32),
             pltpu.VMEM((slots, 8, 128), jnp.float32),
             pltpu.VMEM((N_Z, 8, 128), jnp.float32),
+            pltpu.VMEM((8, share, order), jnp.bfloat16),
             pltpu.VMEM((1, 128), jnp.float32),
             pltpu.VMEM((1, 128), jnp.int32),
             pltpu.SMEM((1, 128), jnp.int32),
-            dma((4,)),
+            dma((7,)),
             dma((RING,)),
             dma((2, 2)),
             dma,
-            dma((66,)),
-            dma((66,)),
+            dma((74,)),
+            dma((74,)),
             dma((2, 4, RING)),
             dma((2, 4, RING)),
             dma((N_Z,)),

time: 107 us -> 105 us (0.981)
  Pallas kernels: 107 us -> 104 us
    pallas_call x1, Pallas kernels: 103 us -> 101 us  [step(): pl.pallas_call(step_kernel, out_shape=(pltpu.VMEM((slots, *block), jnp.bf...]
where the time goes in v6:
time: 105 us; the launch traced here: 104 us
  Pallas kernels  104 us (99%)
    pallas_call x1, Pallas kernels, step(): pl.pallas_call(step_kernel, out_shape=(pltpu.VMEM((slots, *block), jnp.bf...  101 us
    pallas_call x1, Pallas kernels, apply_scale(): pl.pallas_call(scale_kernel, out_shape=jax.ShapeDtypeStruct(x.shape, jnp....  3.83 us

profile of v6, /device:TPU:1, one launch (start us, length us, event | category | flops | bytes accessed | tf_op | source)
XLA Modules:
  0.0 104.4 jit_solution(16941951394332761907)
XLA Ops:
  0.0 100.6 %shard_map.64 = (bf16[64,256,256]{2,1,0:T(8,128)(2,1)S(1)}, f32[64,128]{1,0:T(8,128)S(1)}) custom-call(s32[1,1024]{1,0:T(1,128)} %bitcast.10, bf16[32,256,256]{2,1,0:T(8,128)(2,1)} %grads_hbm.1, bf16[64,32,256]{2,1,0:T(8,128)(2,1)} %bitcast.9, bf16[64,256,256]{2,1,0:T(8,128)(2,1)} %bitcast.6, f32[64,32,256]{2,1,0:T(8,128)} %bitcast.7, f32[64,32,256]{2,1,0:T(8,128)} %bitcast.8), custom_call_target="tpu_custom_call" | custom-call | flops 4294967296 | bytes 400000000 | tf_op jit(solution)/shard_map/pallas_call | solution.py:445
  100.6 3.8 %shard_map.65 = bf16[64,256,256]{2,1,0:T(8,128)(2,1)} custom-call(bf16[64,256,256]{2,1,0:T(8,128)(2,1)S(1)} %get-tuple-element.7.x, f32[64,128]{1,0:T(8,128)S(1)} %get-tuple-element.8.scale), custom_call_target="tpu_custom_call" | custom-call | tf_op jit(solution)/shard_map/pallas_call | solution.py:533

commit v7 on v6

--- a/solution.py
+++ b/solution.py
@@ -11,10 +11,9 @@
 N_Y, N_X, N_C = 4, 4, 2
 N_DP = N_Y * N_X * N_C
 N_Z = 8
-GROUP = 4
 RING = 4
 SIGNS = (1, -1)
-LIMIT = 50
+LIMIT = 48
 
 NEAR, NEAR_LONG, BESIDE, AWAY_LONG, AWAY, BESIDE_CROSS, BESIDE_LONG = range(7)
 START = (0, 12, 16, 28, 32, 44, 56, 64)
@@ -33,11 +32,19 @@
     return lax.rem(g // 2, 2), first, 3 - 2 * low, g // 4 if kind == BESIDE_LONG else int(kind == BESIDE_CROSS)
 
 
+def slot_at(me, kind, pos):
+    y, x, c = me // (N_X * N_C), (me // N_C) % N_X, me % N_C
+    half, first, second, dc = decode(kind, pos - START[kind])
+    dy, dx = second + half * (first - second), first + half * (second - first)
+    source = lax.rem(y + dy, N_Y) * (N_X * N_C) + lax.rem(x + dx, N_X) * N_C + lax.rem(c + dc, N_C)
+    return 2 * source + half
+
+
 def step_kernel(
-    owner, grads_hbm, left_hbm, right_hbm, mone_hbm, mtwo_hbm, recv_v, scale_out,
+    owner, grads_hbm, left_hbm, right_hbm, mone_hbm, mtwo_hbm, recv_v, left_late, right_late, scale_out,
     grads_v, out_v, stage_v, pass_v, relay_v, left_v, right_v, mone_v, mtwo_v,
     adam_v, square_v, tiles_v, strip_v, live_v, idx_v, idx,
-    load_sems, left_sems, own_sems, idx_sem, send_sems, recv_sems, ring_send, ring_recv, zsend, zrecv,
+    load_sems, left_sems, own_sems, late_sems, idx_sem, send_sems, recv_sems, ring_send, ring_recv, zsend, zrecv,
 ):
     me, z = lax.axis_index("dp"), lax.axis_index("replica")
     per_shard, order = grads_hbm.shape[0], grads_hbm.shape[1]
@@ -55,8 +62,7 @@
         return at(second + half * (first - second), first + half * (second - first), dc)
 
     def slot_of(kind, pos):
-        half, first, second, dc = decode(kind, pos - START[kind])
-        return 2 * along(half, first, second, dc) + half
+        return slot_at(me, kind, pos)
 
     quarter = per_shard // 4
     grad_loads = [
@@ -213,16 +219,13 @@
         values = values[:, :128] + values[:, 128:]
         return jnp.sum(values.reshape(values.shape[0] // 8, 8, 128), axis=0)
 
-    def in_fours(kind, some, only=None):
+    def in_fours(kind, some):
         def one(i, carry):
             places = [START[kind] + 4 * i + j for j in range(4)]
             some(places, [slot_of(kind, pos) for pos in places])
             return carry
 
-        if only is None:
-            lax.fori_loop(0, (START[kind + 1] - START[kind]) // 4, one, 0)
-        else:
-            one(only, 0)
+        lax.fori_loop(0, (START[kind + 1] - START[kind]) // 4, one, 0)
 
     def square_ratio(grad, k):
         grad32 = grad.astype(jnp.float32)
@@ -231,25 +234,25 @@
         ratio = moment_one / (jnp.sqrt(moment_two) + 1e-08)
         adam_v[k] = fold(ratio * ratio)
 
-    def absorb(kind, only=None):
+    def absorb(kind):
         def some(places, ks):
-            if kind != BESIDE_LONG:
-                for pos, k in zip(places, ks):
-                    square_ratio(recv_v[pos, rows, :], k)
+            for pos, k in zip(places, ks):
+                square_ratio(recv_v[pos, rows, :], k)
             for pos, k in zip(places, ks):
                 product = jnp.dot(recv_v[pos], right_v[k], preferred_element_type=jnp.float32)
                 recv_v[pos] = product.astype(jnp.bfloat16)
 
-        in_fours(kind, some, only)
+        in_fours(kind, some)
 
     def adam_of_strips():
         def some(places, ks):
             for pos, k in zip(places, ks):
                 square_ratio(strip_v[pos - START[BESIDE_LONG]], k)
+                square_v[k] = jnp.zeros((8, 128), jnp.float32)
 
         in_fours(BESIDE_LONG, some)
 
-    def finish(kind, only=None):
+    def finish(kind):
         def some(places, ks):
             for pos, k in zip(places, ks):
                 precond = jnp.dot(
@@ -258,7 +261,7 @@
                 square_v[k] = fold(precond * precond)
                 recv_v[pos] = precond.astype(jnp.bfloat16)
 
-        in_fours(kind, some, only)
+        in_fours(kind, some)
 
     def count_live():
         shard = lax.broadcasted_iota(jnp.int32, (owner.shape[1], 128), 0) // per_shard
@@ -349,6 +352,13 @@
         passed[h, 1, part].start()
     for load in loads:
         load.wait()
+    first_late = START[BESIDE_LONG]
+    to_late = [
+        pltpu.make_async_copy(right_v.at[slot_of(BESIDE_LONG, first_late + i)], right_late.at[i], late_sems.at[i])
+        for i in range(slots - first_late)
+    ]
+    for copy in to_late:
+        copy.start()
     for m in range(2):
         for h in range(2):
             own[h, m].wait()
@@ -412,13 +422,31 @@
     pass_on(3, 2)
     finish(AWAY)
     pass_on(3, 3)
+    to_late.append(
+        pltpu.make_async_copy(
+            left_v.at[:, pl.ds(first_late, slots - first_late)], left_late, late_sems.at[slots - first_late]
+        )
+    )
+    to_late[-1].start()
     finish(BESIDE_CROSS)
+    sum_pre = by_lane(square_v[...])
+    for dz in range(1, N_Z):
+        tell(dz).wait()
+    sum_adam = jnp.sum(tiles_v[...], axis=0)[:1]
+    lane = lax.broadcasted_iota(jnp.int32, (1, 128), 1)
+    dy = lax.rem(lane // (2 * N_X * N_C) - y + 2 * N_Y, N_Y)
+    dx = lax.rem(lax.rem(lane // (2 * N_C), N_X) - x + N_X, N_X)
+    odd = lax.rem(lane, 2) == 1
+    later = (jnp.where(odd, dy, dx) == 2) & (lax.rem(jnp.where(odd, dx, dy), 2) == 1)
+    norm = live_v[...] * jnp.sqrt(sum_adam / total)
+    scale = jnp.where(later, norm, norm / jnp.sqrt(sum_pre / total + 1e-06))
+    by_row = jnp.where(diagonal, jnp.broadcast_to(scale, (slots, 128)), 0.0)
+    scale_out[...] = jnp.broadcast_to(jnp.sum(by_row, axis=1, keepdims=True), (slots, 128))
+    for copy in to_late:
+        copy.wait()
     for dc in range(N_C):
         for h, part in every:
             ahead[h, 1, part, dc].wait_recv()
-        absorb(BESIDE_LONG, dc)
-        finish(BESIDE_LONG, dc)
-    sum_pre = by_lane(square_v[...])
     for group in (via, straight, onward, far, ahead, inside, passed, strip):
         for copy in group.values():
             copy.wait_send()
@@ -427,18 +455,13 @@
             for part in range(2):
                 if travels(part, t, chunk):
                     ring_out(part, t, chunk).wait_send()
-    for dz in range(1, N_Z):
-        tell(dz).wait()
-    sum_adam = jnp.sum(tiles_v[...], axis=0)[:1]
-    scale = live_v[...] * (jnp.sqrt(sum_adam / total) / jnp.sqrt(sum_pre / total + 1e-06))
-    by_row = jnp.where(diagonal, jnp.broadcast_to(scale, (slots, 128)), 0.0)
-    scale_out[...] = jnp.broadcast_to(jnp.sum(by_row, axis=1, keepdims=True), (slots, 128))
 
 
 def step(owner, grads, left, right, mone, mtwo):
     per_shard, order, _ = grads.shape
     slots, share, _ = mone.shape
     block = (order, order)
+    late = slots - START[BESIDE_LONG]
     anywhere = pl.BlockSpec(memory_space=pl.ANY)
     vmem = pl.BlockSpec(memory_space=pltpu.VMEM)
     dma = pltpu.SemaphoreType.DMA
@@ -446,10 +469,12 @@
         step_kernel,
         out_shape=(
             pltpu.VMEM((slots, *block), jnp.bfloat16),
+            pltpu.VMEM((N_Z, late, share, order), jnp.bfloat16),
+            pltpu.VMEM((late, *block), jnp.bfloat16),
             pltpu.VMEM((slots, 128), jnp.float32),
         ),
         in_specs=[vmem] + [anywhere] * 5,
-        out_specs=(vmem, vmem),
+        out_specs=(vmem, vmem, vmem, vmem),
         scratch_shapes=[
             pltpu.VMEM((per_shard + 1, *block), jnp.bfloat16),
             pltpu.VMEM((2, 3, 8, *block), jnp.bfloat16),
@@ -470,6 +495,7 @@
             dma((7,)),
             dma((RING,)),
             dma((2, 2)),
+            dma((late + 1,)),
             dma,
             dma((74,)),
             dma((74,)),
@@ -487,67 +513,83 @@
     )(owner, grads, left, right, mone, mtwo)
 
 
-def place_of(me, slot):
-    y, x, c = me // (N_X * N_C), (me // N_C) % N_X, me % N_C
-    source, half = slot // 2, lax.rem(slot, 2)
-    dy = lax.rem(source // (N_X * N_C) - y + N_Y, N_Y)
-    dx = lax.rem(lax.rem(source // N_C, N_X) - x + N_X, N_X)
-    dc = lax.rem(source + c, N_C)
-    first, second = dx + half * (dy - dx), dy + half * (dx - dy)
-    d = lax.rem(first + 1, 4)
-    g, beside = half * 2 + dc, half * 2 + (3 - second) // 2
-    near = jnp.where(d == 3, START[NEAR_LONG] + g, START[NEAR] + 3 * g + d)
-    away = jnp.where(d == 3, START[AWAY_LONG] + g, START[AWAY] + 3 * g + d)
-    cross = START[BESIDE] + dc * (START[BESIDE_CROSS] - START[BESIDE])
-    middle = jnp.where(d == 3, START[BESIDE_LONG] + dc * 4 + beside, cross + 3 * beside + d)
-    return jnp.where(second == 0, near, jnp.where(second == 2, away, middle))
-
-
-def scale_kernel(x, scale, out, ready, sems):
+def scale_kernel(x, left, right, scale, out, ready, sems):
     me = lax.axis_index("dp")
-
-    def copy(i):
-        some = pl.ds(GROUP * i, GROUP)
-        return pltpu.make_async_copy(ready.at[some], out.at[some], sems.at[i])
-
-    def one(i, carry):
-        for j in range(GROUP):
-            k = GROUP * i + j
-            row = scale[pl.ds(k, 1), :]
-            factor = jnp.concatenate([row, row], axis=1)
-            ready[k] = (x[place_of(me, k)].astype(jnp.float32) * factor).astype(jnp.bfloat16)
-        copy(i).start()
-        return carry
-
-    def settle(i, carry):
-        copy(i).wait()
-        return carry
-
-    steps = x.shape[0] // GROUP
-    lax.fori_loop(0, steps, one, 0)
-    lax.fori_loop(0, steps, settle, 0)
-
-
-def apply_scale(x, scale):
-    vmem = pl.BlockSpec(memory_space=pltpu.VMEM)
+    order = x.shape[1]
+    last = START[BESIDE_LONG]
+
+    def copy(kind, pos):
+        return pltpu.make_async_copy(ready.at[pos], out.at[slot_at(me, kind, pos)], sems.at[pos])
+
+    def row(kind, pos):
+        return scale[pl.ds(slot_at(me, kind, pos), 1), :]
+
+    def in_fours(kind, some):
+        def one(i, carry):
+            places = [START[kind] + 4 * i + j for j in range(4)]
+            some(places)
+            for pos in places:
+                copy(kind, pos).start()
+            return carry
+
+        lax.fori_loop(0, (START[kind + 1] - START[kind]) // 4, one, 0)
+
+    def store(pos, values, factor):
+        ready[pos] = (values * jnp.concatenate([factor, factor], axis=1)).astype(jnp.bfloat16)
+
+    for kind in range(BESIDE_LONG):
+
+        def scaled(places):
+            for pos in places:
+                store(pos, x[pos].astype(jnp.float32), row(kind, pos))
+
+        in_fours(kind, scaled)
+
+    def whole(places):
+        halves = [
+            jnp.dot(
+                left[:, pos - last].reshape(order, order), x[pos], preferred_element_type=jnp.float32
+            ).astype(jnp.bfloat16)
+            for pos in places
+        ]
+        preconds = [
+            jnp.dot(half, right[pos - last], preferred_element_type=jnp.float32)
+            for pos, half in zip(places, halves)
+        ]
+        for pos, precond in zip(places, preconds):
+            mean = jnp.sum(precond * precond, axis=(0, 1), keepdims=True) / float(order * order) + 1e-06
+            store(pos, precond, row(BESIDE_LONG, pos) / jnp.sqrt(mean))
+
+    in_fours(BESIDE_LONG, whole)
+    for kind in range(BESIDE_LONG + 1):
+
+        def settle(pos, carry):
+            copy(kind, pos).wait()
+            return carry
+
+        lax.fori_loop(START[kind], START[kind + 1], settle, 0)
+
+
+def apply_scale(x, left, right, scale):
+    vmem, anywhere = pl.BlockSpec(memory_space=pltpu.VMEM), pl.BlockSpec(memory_space=pl.ANY)
     return pl.pallas_call(
         scale_kernel,
         out_shape=jax.ShapeDtypeStruct(x.shape, jnp.bfloat16),
-        in_specs=[vmem, vmem],
-        out_specs=pl.BlockSpec(memory_space=pl.ANY),
+        in_specs=[vmem] * 4,
+        out_specs=anywhere,
         scratch_shapes=[
             pltpu.VMEM(x.shape, jnp.bfloat16),
-            pltpu.SemaphoreType.DMA((x.shape[0] // GROUP,)),
+            pltpu.SemaphoreType.DMA((x.shape[0],)),
         ],
         compiler_params=pltpu.CompilerParams(vmem_limit_bytes=24 * 2**20),
-    )(x, scale)
+    )(x, left, right, scale)
 
 
 def per_device(grads, owner, left_root, right_root, first_moment, second_moment):
-    x, scale = step(
+    x, left, right, scale = step(
         owner.reshape(1, -1), grads, left_root[0], right_root[0], first_moment[0], second_moment[0]
     )
-    return apply_scale(x, scale)[None]
+    return apply_scale(x, left, right, scale)[None]
 
 
 def solution(mesh):

time: 105 us -> 105 us (level)
  no operation moved by 1% of the time
where the time goes in v7:
time: 105 us; the launch traced here: 104 us
  Pallas kernels  104 us (99%)
    pallas_call x1, Pallas kernels, step(): pl.pallas_call(step_kernel, out_shape=(pltpu.VMEM((slots, *block), jnp.bf...  100 us
    pallas_call x1, Pallas kernels, apply_scale(): pl.pallas_call(scale_kernel, out_shape=jax.ShapeDtypeStruct(x.shape, jnp....  4.22 us

profile of v7, /device:TPU:1, one launch (start us, length us, event | category | flops | bytes accessed | tf_op | source)
XLA Modules:
  0.0 104.4 jit_solution(3284016332254838754)
XLA Ops:
  0.0 100.2 %shard_map.64 = (bf16[64,256,256]{2,1,0:T(8,128)(2,1)S(1)}, bf16[8,8,32,256]{3,2,1,0:T(8,128)(2,1)S(1)}, bf16[8,256,256]{2,1,0:T(8,128)(2,1)S(1)}, f32[64,128]{1,0:T(8,128)S(1)}) custom-call(s32[1,1024]{1,0:T(1,128)} %bitcast.10, bf16[32,256,256]{2,1,0:T(8,128)(2,1)} %grads_hbm.1, bf16[64,32,256]{2,1,0:T(8,128)(2,1)} %bitcast.9, ...), custom_call_target="tpu_custom_call" | custom-call | flops 4294967296 | bytes 400000000 | tf_op jit(solution)/shard_map/pallas_call | solution.py:468
  100.2 4.2 %shard_map.65 = bf16[64,256,256]{2,1,0:T(8,128)(2,1)} custom-call(bf16[64,256,256]{2,1,0:T(8,128)(2,1)S(1)} %get-tuple-element.9.x, bf16[8,8,32,256]{3,2,1,0:T(8,128)(2,1)S(1)} %get-tuple-element.10.left, bf16[8,256,256]{2,1,0:T(8,128)(2,1)S(1)} %get-tuple-element.11.right, f32[64,128]{1,0:T(8,128)S(1)} %get-tuple-element.12.scale), custom_call_target="tpu_custom_call" | custom-call | tf_op jit(solution)/shard_map/pallas_call | solution.py:575

commit v8 on v7

--- a/solution.py
+++ b/solution.py
@@ -234,13 +234,13 @@
         ratio = moment_one / (jnp.sqrt(moment_two) + 1e-08)
         adam_v[k] = fold(ratio * ratio)
 
-    def absorb(kind):
+    def absorb(kind, adam=True, product=True):
         def some(places, ks):
-            for pos, k in zip(places, ks):
+            for pos, k in zip(places, ks) if adam else ():
                 square_ratio(recv_v[pos, rows, :], k)
-            for pos, k in zip(places, ks):
-                product = jnp.dot(recv_v[pos], right_v[k], preferred_element_type=jnp.float32)
-                recv_v[pos] = product.astype(jnp.bfloat16)
+            for pos, k in zip(places, ks) if product else ():
+                right = jnp.dot(recv_v[pos], right_v[k], preferred_element_type=jnp.float32)
+                recv_v[pos] = right.astype(jnp.bfloat16)
 
         in_fours(kind, some)
 
@@ -344,6 +344,9 @@
     pass_on(1, 1, 2)
     for h, part in every:
         onward[h, 0, part].wait_recv()
+    for dc in range(N_C):
+        for h, part in every:
+            strip[h, part, dc].start()
     for h in range(2):
         inside[h, 1].start()
         own[h, 1].start()
@@ -373,9 +376,6 @@
         ahead[h, 0, part, 1].start()
     for dc in range(N_C):
         for h, part in every:
-            strip[h, part, dc].start()
-    for dc in range(N_C):
-        for h, part in every:
             ahead[h, 1, part, dc].start()
     pass_on(2, 0, 1)
     for h, part in every:
@@ -388,6 +388,10 @@
     pass_on(2, 2, 3)
     for h, part in every:
         passed[h, 0, part].wait_recv()
+    for dc in range(N_C):
+        for h, part in every:
+            strip[h, part, dc].wait_recv()
+    adam_of_strips()
     absorb(AWAY)
     pass_on(3, 0, 1)
     for kind in (NEAR, NEAR_LONG, BESIDE):
@@ -399,12 +403,7 @@
     finish(AWAY_LONG)
     for h, part in every:
         ahead[h, 0, part, 1].wait_recv()
-    absorb(BESIDE_CROSS)
-    for dc in range(N_C):
-        for h, part in every:
-            strip[h, part, dc].wait_recv()
-    adam_of_strips()
-
+    absorb(BESIDE_CROSS, product=False)
     tiles_v[0] = jnp.broadcast_to(by_lane(adam_v[...]), (8, 128))
 
     def tell(dz):
@@ -419,6 +418,7 @@
 
     for dz in range(1, N_Z):
         tell(dz).start()
+    absorb(BESIDE_CROSS, adam=False)
     pass_on(3, 2)
     finish(AWAY)
     pass_on(3, 3)

time: 105 us -> 104 us (level)
  no operation moved by 1% of the time
where the time goes in v8:
time: 104 us
  Pallas kernels  104 us (100%)
    pallas_call x1, Pallas kernels, step(): pl.pallas_call(step_kernel, out_shape=(pltpu.VMEM((slots, *block), jnp.bf...  99.8 us
    pallas_call x1, Pallas kernels, apply_scale(): pl.pallas_call(scale_kernel, out_shape=jax.ShapeDtypeStruct(x.shape, jnp....  4.22 us

profile of v8, /device:TPU:1, one launch (start us, length us, event | category | flops | bytes accessed | tf_op | source)
XLA Modules:
  0.0 104.0 jit_solution(14512305479960932518)
XLA Ops:
  0.0 99.8 %shard_map.64 = (bf16[64,256,256]{2,1,0:T(8,128)(2,1)S(1)}, bf16[8,8,32,256]{3,2,1,0:T(8,128)(2,1)S(1)}, bf16[8,256,256]{2,1,0:T(8,128)(2,1)S(1)}, f32[64,128]{1,0:T(8,128)S(1)}) custom-call(s32[1,1024]{1,0:T(1,128)} %bitcast.10, bf16[32,256,256]{2,1,0:T(8,128)(2,1)} %grads_hbm.1, bf16[64,32,256]{2,1,0:T(8,128)(2,1)} %bitcast.9, ...), custom_call_target="tpu_custom_call" | custom-call | flops 4294967296 | bytes 400000000 | tf_op jit(solution)/shard_map/pallas_call | solution.py:468
  99.8 4.2 %shard_map.65 = bf16[64,256,256]{2,1,0:T(8,128)(2,1)} custom-call(bf16[64,256,256]{2,1,0:T(8,128)(2,1)S(1)} %get-tuple-element.9.x, bf16[8,8,32,256]{3,2,1,0:T(8,128)(2,1)S(1)} %get-tuple-element.10.left, bf16[8,256,256]{2,1,0:T(8,128)(2,1)S(1)} %get-tuple-element.11.right, f32[64,128]{1,0:T(8,128)S(1)} %get-tuple-element.12.scale), custom_call_target="tpu_custom_call" | custom-call | tf_op jit(solution)/shard_map/pallas_call | solution.py:575

commit v9 on v8

--- a/solution.py
+++ b/solution.py
@@ -43,7 +43,7 @@
 def step_kernel(
     owner, grads_hbm, left_hbm, right_hbm, mone_hbm, mtwo_hbm, recv_v, left_late, right_late, scale_out,
     grads_v, out_v, stage_v, pass_v, relay_v, left_v, right_v, mone_v, mtwo_v,
-    adam_v, square_v, tiles_v, strip_v, live_v, idx_v, idx,
+    adam_v, square_v, tiles_v, live_v, idx_v, idx,
     load_sems, left_sems, own_sems, late_sems, idx_sem, send_sems, recv_sems, ring_send, ring_recv, zsend, zrecv,
 ):
     me, z = lax.axis_index("dp"), lax.axis_index("replica")
@@ -124,17 +124,19 @@
             device_id=(target, plane), device_id_type=MESH,
         )
 
-    def place(kind, g):
+    def place(kind, g, some=slice(None)):
         n = 1 if kind in (NEAR_LONG, AWAY_LONG, BESIDE_LONG) else 3
-        return recv_v.at[pl.ds(START[kind] + n * g, n)]
+        return recv_v.at[pl.ds(START[kind] + n * g, n), some]
 
     parity = lax.rem(z, 2)
     half_rows = pl.ds(pl.multiple_of(parity * (order // 2), order // 2), order // 2)
     other_rows = pl.ds(pl.multiple_of((1 - parity) * (order // 2), order // 2), order // 2)
     pieces = (pl.ds(0, 3), pl.ds(3, 1))
     via, straight, onward = {}, {}, {}
-    far, ahead, inside, passed, own, swap, swapped, strip = {}, {}, {}, {}, {}, {}, {}, {}
+    far, ahead, inside, passed, own, swap, swapped, halves = {}, {}, {}, {}, {}, {}, {}, {}
     rows = pl.ds(pl.multiple_of(z * share, share), share)
+    upper = z // (N_Z // 2) * (order // 2)
+    in_order = [pl.ds(pl.multiple_of(r, order // 2), order // 2) for r in (upper, order // 2 - upper)]
     for h in range(2):
         for part, sign in enumerate(SIGNS):
             there = along(h, sign, 0, 0)
@@ -153,24 +155,30 @@
             far[h, 0, part] = message(
                 stage_v.at[h, pieces[0], 3 + part], relay_v.at[h, part, pieces[0]], there
             )
-            passed[h, 0, part] = message(relay_v.at[h, part, pieces[0]], place(AWAY, h * 2 + part), last)
+            for q, some in enumerate(in_order):
+                halves[AWAY, q, h, part] = message(
+                    relay_v.at[h, part, pieces[0], some], place(AWAY, h * 2 + part, some), last
+                )
             far[h, 1, part] = message(
                 stage_v.at[h, 3, 3 + part, half_rows], relay_v.at[h, part, 3, half_rows], there
             )
-            passed[h, 1, part] = message(
+            passed[h, part] = message(
                 relay_v.at[h, part, 3, half_rows], recv_v.at[START[AWAY_LONG] + h * 2 + part, half_rows], last
             )
-            for dc in range(N_C):
-                strip[h, part, dc] = message(
-                    stage_v.at[h, 3, PACKED.index((sign % 4, dc)), rows],
-                    strip_v.at[dc * 4 + h * 2 + part],
-                    along(h, 0, sign, dc),
+            beside = [PACKED.index((sign % 4, dc)) for dc in range(N_C)]
+            ahead[h, part] = message(
+                stage_v.at[h, pieces[0], beside[0]], place(BESIDE, h * 2 + part), along(h, 0, sign, 0)
+            )
+            for q, some in enumerate(in_order):
+                halves[BESIDE_CROSS, q, h, part] = message(
+                    stage_v.at[h, pieces[0], beside[1], some],
+                    place(BESIDE_CROSS, h * 2 + part, some),
+                    along(h, 0, sign, 1),
                 )
-            for m, piece in enumerate(pieces):
                 for dc in range(N_C):
-                    ahead[h, m, part, dc] = message(
-                        stage_v.at[h, piece, PACKED.index((sign % 4, dc))],
-                        place((BESIDE, BESIDE_CROSS)[dc], h * 2 + part) if m == 0 else place(BESIDE_LONG, dc * 4 + h * 2 + part),
+                    halves[BESIDE_LONG, q, h, part, dc] = message(
+                        stage_v.at[h, pieces[1], beside[dc], some],
+                        place(BESIDE_LONG, dc * 4 + h * 2 + part, some),
                         along(h, 0, sign, dc),
                     )
         for m, piece in enumerate(pieces):
@@ -203,12 +211,12 @@
     def travels(part, t, chunk):
         return t < 3 or chunk % 2 == part
 
-    def pass_on(t, *chunks):
+    def pass_on(t, *chunks, forward=True):
         for chunk in chunks:
             for part in range(2):
                 if travels(part, t, chunk):
                     ring_in(part, t, chunk).wait_recv()
-                if t < 3 and travels(part, t + 1, chunk):
+                if forward and t < 3 and travels(part, t + 1, chunk):
                     ring_out(part, t + 1, chunk).start()
 
     def begin(chunk):
@@ -238,19 +246,13 @@
         def some(places, ks):
             for pos, k in zip(places, ks) if adam else ():
                 square_ratio(recv_v[pos, rows, :], k)
+                if kind == BESIDE_LONG:
+                    square_v[k] = jnp.zeros((8, 128), jnp.float32)
             for pos, k in zip(places, ks) if product else ():
                 right = jnp.dot(recv_v[pos], right_v[k], preferred_element_type=jnp.float32)
                 recv_v[pos] = right.astype(jnp.bfloat16)
 
         in_fours(kind, some)
-
-    def adam_of_strips():
-        def some(places, ks):
-            for pos, k in zip(places, ks):
-                square_ratio(strip_v[pos - START[BESIDE_LONG]], k)
-                square_v[k] = jnp.zeros((8, 128), jnp.float32)
-
-        in_fours(BESIDE_LONG, some)
 
     def finish(kind):
         def some(places, ks):
@@ -311,48 +313,54 @@
     for h, part in every:
         via[h, 1, part].wait_recv()
         onward[h, 1, part].start()
-    for b in range(2):
-        for h, part in every:
+    for h, part in every:
+        for b in range(2):
             pack(h, SIGNS[part], thirds[b], out_v.at[h, part])
-            straight[h, b, part].start()
     for h in range(2):
         pack(h, 0, range(8), stage_v.at[h, 1])
     count_live()
 
+    def halves_of(kind, q):
+        return [copy for key, copy in halves.items() if key[:2] == (kind, q)]
+
     pass_on(0, 0)
+    for h, part in every:
+        onward[h, 1, part].wait_recv()
+        far[h, 1, part].start()
+    for b in range(2):
+        for h, part in every:
+            straight[h, b, part].start()
     for h, part in every:
         via[h, 0, part].wait_recv()
         onward[h, 0, part].start()
     pass_on(0, 1)
     for h, part in every:
-        onward[h, 1, part].wait_recv()
-        far[h, 1, part].start()
-    for h, part in every:
         straight[h, 2, part].wait_recv()
     for h, part in every:
         far[h, 0, part].start()
+    for h, part in every:
+        far[h, 1, part].wait_recv()
+        passed[h, part].start()
     pass_on(0, 2, 3)
     pass_on(1, 0)
     for h, part in every:
         for b in range(2):
             straight[h, b, part].wait_recv()
     for h, part in every:
-        ahead[h, 0, part, 0].start()
+        ahead[h, part].start()
     for h in range(2):
         inside[h, 0].start()
         own[h, 0].start()
     pass_on(1, 1, 2)
     for h, part in every:
         onward[h, 0, part].wait_recv()
-    for dc in range(N_C):
-        for h, part in every:
-            strip[h, part, dc].start()
     for h in range(2):
         inside[h, 1].start()
         own[h, 1].start()
-    for h, part in every:
-        far[h, 1, part].wait_recv()
-        passed[h, 1, part].start()
+    for h in range(2):
+        for part in range(2):
+            passed[h, part].wait_recv()
+        swap[h].start()
     for load in loads:
         load.wait()
     first_late = START[BESIDE_LONG]
@@ -371,39 +379,23 @@
     pass_on(1, 3)
     for h, part in every:
         far[h, 0, part].wait_recv()
-        passed[h, 0, part].start()
-    for h, part in every:
-        ahead[h, 0, part, 1].start()
-    for dc in range(N_C):
-        for h, part in every:
-            ahead[h, 1, part, dc].start()
+    for q in range(2):
+        for kind in (AWAY, BESIDE_CROSS, BESIDE_LONG):
+            for copy in halves_of(kind, q):
+                copy.start()
     pass_on(2, 0, 1)
-    for h, part in every:
-        ahead[h, 0, part, 0].wait_recv()
-    for h in range(2):
-        for part in range(2):
-            passed[h, 1, part].wait_recv()
-        swap[h].start()
-    absorb(BESIDE)
-    pass_on(2, 2, 3)
-    for h, part in every:
-        passed[h, 0, part].wait_recv()
-    for dc in range(N_C):
-        for h, part in every:
-            strip[h, part, dc].wait_recv()
-    adam_of_strips()
-    absorb(AWAY)
-    pass_on(3, 0, 1)
-    for kind in (NEAR, NEAR_LONG, BESIDE):
-        finish(kind)
     for h in range(2):
         swapped[h].wait_recv()
         swap[h].wait_send()
     absorb(AWAY_LONG)
-    finish(AWAY_LONG)
-    for h, part in every:
-        ahead[h, 0, part, 1].wait_recv()
-    absorb(BESIDE_CROSS, product=False)
+    for h, part in every:
+        ahead[h, part].wait_recv()
+    absorb(BESIDE)
+    pass_on(2, 2, forward=False)
+    for kind in (AWAY, BESIDE_CROSS, BESIDE_LONG):
+        for copy in halves_of(kind, 0):
+            copy.wait_recv()
+        absorb(kind, product=False)
     tiles_v[0] = jnp.broadcast_to(by_lane(adam_v[...]), (8, 128))
 
     def tell(dz):
@@ -418,6 +410,19 @@
 
     for dz in range(1, N_Z):
         tell(dz).start()
+    pass_on(2, 3, forward=False)
+    for chunk in (2, 3):
+        for part in range(2):
+            if travels(part, 3, chunk):
+                ring_out(part, 3, chunk).start()
+    for copy in halves_of(AWAY, 1):
+        copy.wait_recv()
+    absorb(AWAY, adam=False)
+    pass_on(3, 0, 1)
+    for kind in (NEAR, NEAR_LONG, BESIDE, AWAY_LONG):
+        finish(kind)
+    for copy in halves_of(BESIDE_CROSS, 1):
+        copy.wait_recv()
     absorb(BESIDE_CROSS, adam=False)
     pass_on(3, 2)
     finish(AWAY)
@@ -444,10 +449,9 @@
     scale_out[...] = jnp.broadcast_to(jnp.sum(by_row, axis=1, keepdims=True), (slots, 128))
     for copy in to_late:
         copy.wait()
-    for dc in range(N_C):
-        for h, part in every:
-            ahead[h, 1, part, dc].wait_recv()
-    for group in (via, straight, onward, far, ahead, inside, passed, strip):
+    for copy in halves_of(BESIDE_LONG, 1):
+        copy.wait_recv()
+    for group in (via, straight, onward, far, ahead, inside, passed, halves):
         for copy in group.values():
             copy.wait_send()
     for t in range(4):
@@ -488,7 +492,6 @@
             pltpu.VMEM((slots, 8, 128), jnp.float32),
             pltpu.VMEM((slots, 8, 128), jnp.float32),
             pltpu.VMEM((N_Z, 8, 128), jnp.float32),
-            pltpu.VMEM((8, share, order), jnp.bfloat16),
             pltpu.VMEM((1, 128), jnp.float32),
             pltpu.VMEM((1, 128), jnp.int32),
             pltpu.SMEM((1, 128), jnp.int32),
@@ -497,8 +500,8 @@
             dma((2, 2)),
             dma((late + 1,)),
             dma,
-            dma((74,)),
-            dma((74,)),
+            dma((82,)),
+            dma((82,)),
             dma((2, 4, RING)),
             dma((2, 4, RING)),
             dma((N_Z,)),
@@ -524,26 +527,25 @@
     def row(kind, pos):
         return scale[pl.ds(slot_at(me, kind, pos), 1), :]
 
-    def in_fours(kind, some):
+    def in_groups(kind, n, some):
         def one(i, carry):
-            places = [START[kind] + 4 * i + j for j in range(4)]
+            places = [START[kind] + n * i + j for j in range(n)]
             some(places)
             for pos in places:
                 copy(kind, pos).start()
             return carry
 
-        lax.fori_loop(0, (START[kind + 1] - START[kind]) // 4, one, 0)
+        lax.fori_loop(0, (START[kind + 1] - START[kind]) // n, one, 0)
 
     def store(pos, values, factor):
         ready[pos] = (values * jnp.concatenate([factor, factor], axis=1)).astype(jnp.bfloat16)
 
-    for kind in range(BESIDE_LONG):
-
+    def scale_all(kind):
         def scaled(places):
             for pos in places:
                 store(pos, x[pos].astype(jnp.float32), row(kind, pos))
 
-        in_fours(kind, scaled)
+        in_groups(kind, 4, scaled)
 
     def whole(places):
         halves = [
@@ -560,7 +562,10 @@
             mean = jnp.sum(precond * precond, axis=(0, 1), keepdims=True) / float(order * order) + 1e-06
             store(pos, precond, row(BESIDE_LONG, pos) / jnp.sqrt(mean))
 
-    in_fours(BESIDE_LONG, whole)
+    for kind in (NEAR, NEAR_LONG, BESIDE, AWAY_LONG, AWAY):
+        scale_all(kind)
+    in_groups(BESIDE_LONG, 8, whole)
+    scale_all(BESIDE_CROSS)
     for kind in range(BESIDE_LONG + 1):
 
         def settle(pos, carry):

time: 104 us -> 108 us (1.038)
  Pallas kernels: 104 us -> 108 us
    pallas_call x1, Pallas kernels: 99.8 us -> 104 us  [step(): pl.pallas_call(step_kernel, out_shape=(pltpu.VMEM((slots, *block), jnp.bf...]
where the time goes in v9:
time: 108 us
  Pallas kernels  108 us (100%)
    pallas_call x1, Pallas kernels, step(): pl.pallas_call(step_kernel, out_shape=(pltpu.VMEM((slots, *block), jnp.bf...  104 us
    pallas_call x1, Pallas kernels, apply_scale(): pl.pallas_call(scale_kernel, out_shape=jax.ShapeDtypeStruct(x.shape, jnp....  4.2 us

profile of v9, /device:TPU:1, one launch (start us, length us, event | category | flops | bytes accessed | tf_op | source)
XLA Modules:
  0.0 107.9 jit_solution(8727676459408536111)
XLA Ops:
  0.0 103.7 %shard_map.64 = (bf16[64,256,256]{2,1,0:T(8,128)(2,1)S(1)}, bf16[8,8,32,256]{3,2,1,0:T(8,128)(2,1)S(1)}, bf16[8,256,256]{2,1,0:T(8,128)(2,1)S(1)}, f32[64,128]{1,0:T(8,128)S(1)}) custom-call(s32[1,1024]{1,0:T(1,128)} %bitcast.10, bf16[32,256,256]{2,1,0:T(8,128)(2,1)} %grads_hbm.1, bf16[64,32,256]{2,1,0:T(8,128)(2,1)} %bitcast.9, ...), custom_call_target="tpu_custom_call" | custom-call | flops 4294967296 | bytes 400000000 | tf_op jit(solution)/shard_map/pallas_call | solution.py:472
  103.7 4.2 %shard_map.65 = bf16[64,256,256]{2,1,0:T(8,128)(2,1)} custom-call(bf16[64,256,256]{2,1,0:T(8,128)(2,1)S(1)} %get-tuple-element.9.x, bf16[8,8,32,256]{3,2,1,0:T(8,128)(2,1)S(1)} %get-tuple-element.10.left, bf16[8,256,256]{2,1,0:T(8,128)(2,1)S(1)} %get-tuple-element.11.right, f32[64,128]{1,0:T(8,128)S(1)} %get-tuple-element.12.scale), custom_call_target="tpu_custom_call" | custom-call | tf_op jit(solution)/shard_map/pallas_call | solution.py:580

commit v10 on v8

--- a/solution.py
+++ b/solution.py
@@ -21,23 +21,27 @@
 FULL = (pl.ds(0, 3), pl.ds(5, 3))
 
 
-def decode(kind, q):
-    long = kind in (NEAR_LONG, AWAY_LONG, BESIDE_LONG)
-    d, g = (3, q) if long else (lax.rem(q, 3), q // 3)
-    first, low = lax.rem(d + 3, 4), lax.rem(g, 2)
+LONG = (NEAR_LONG, AWAY_LONG, BESIDE_LONG)
+
+
+def slot_of_group(me, kind, d, g):
+    y, x, c = me // (N_X * N_C), (me // N_C) % N_X, me % N_C
+    first, low = (d + 3) % 4 if isinstance(d, int) else lax.rem(d + 3, 4), lax.rem(g, 2)
     if kind in (NEAR, NEAR_LONG):
-        return g // 2, first, 0, low
-    if kind in (AWAY, AWAY_LONG):
-        return g // 2, first, 2, low
-    return lax.rem(g // 2, 2), first, 3 - 2 * low, g // 4 if kind == BESIDE_LONG else int(kind == BESIDE_CROSS)
-
-
-def slot_at(me, kind, pos):
-    y, x, c = me // (N_X * N_C), (me // N_C) % N_X, me % N_C
-    half, first, second, dc = decode(kind, pos - START[kind])
+        half, second, dc = g // 2, 0, low
+    elif kind in (AWAY, AWAY_LONG):
+        half, second, dc = g // 2, 2, low
+    else:
+        half, second = lax.rem(g // 2, 2), 3 - 2 * low
+        dc = g // 4 if kind == BESIDE_LONG else int(kind == BESIDE_CROSS)
     dy, dx = second + half * (first - second), first + half * (second - first)
     source = lax.rem(y + dy, N_Y) * (N_X * N_C) + lax.rem(x + dx, N_X) * N_C + lax.rem(c + dc, N_C)
     return 2 * source + half
+
+
+def slot_at(me, kind, pos):
+    q = pos - START[kind]
+    return slot_of_group(me, kind, 3, q) if kind in LONG else slot_of_group(me, kind, lax.rem(q, 3), q // 3)
 
 
 def step_kernel(
@@ -386,6 +390,11 @@
         swap[h].start()
     absorb(BESIDE)
     pass_on(2, 2, 3)
+    done = [copy for group in (via, straight, onward, far, inside, strip) for copy in group.values()]
+    done += [passed[h, 1, part] for h, part in every] + [ahead[h, 0, part, 0] for h, part in every]
+    done += [ring_out(part, t, chunk) for t in range(2) for chunk in range(RING) for part in range(2)]
+    for copy in done:
+        copy.wait_send()
     for h, part in every:
         passed[h, 0, part].wait_recv()
     for dc in range(N_C):
@@ -418,6 +427,9 @@
 
     for dz in range(1, N_Z):
         tell(dz).start()
+    for chunk in range(RING):
+        for part in range(2):
+            ring_out(part, 2, chunk).wait_send()
     absorb(BESIDE_CROSS, adam=False)
     pass_on(3, 2)
     finish(AWAY)
@@ -447,14 +459,11 @@
     for dc in range(N_C):
         for h, part in every:
             ahead[h, 1, part, dc].wait_recv()
-    for group in (via, straight, onward, far, ahead, inside, passed, strip):
-        for copy in group.values():
-            copy.wait_send()
-    for t in range(4):
-        for chunk in range(RING):
-            for part in range(2):
-                if travels(part, t, chunk):
-                    ring_out(part, t, chunk).wait_send()
+    done = [passed[h, 0, part] for h, part in every] + [ahead[h, 0, part, 1] for h, part in every]
+    done += [ahead[h, 1, part, dc] for dc in range(N_C) for h, part in every]
+    done += [ring_out(part, 3, chunk) for chunk in range(RING) for part in range(2) if travels(part, 3, chunk)]
+    for copy in done:
+        copy.wait_send()
 
 
 def step(owner, grads, left, right, mone, mtwo):
@@ -513,39 +522,37 @@
     )(owner, grads, left, right, mone, mtwo)
 
 
-def scale_kernel(x, left, right, scale, out, ready, sems):
+def scale_kernel(x, left, right, scale, out, ready, sem):
     me = lax.axis_index("dp")
     order = x.shape[1]
     last = START[BESIDE_LONG]
 
-    def copy(kind, pos):
-        return pltpu.make_async_copy(ready.at[pos], out.at[slot_at(me, kind, pos)], sems.at[pos])
-
-    def row(kind, pos):
-        return scale[pl.ds(slot_at(me, kind, pos), 1), :]
-
-    def in_fours(kind, some):
+    def in_groups(kind, some):
         def one(i, carry):
-            places = [START[kind] + 4 * i + j for j in range(4)]
-            some(places)
-            for pos in places:
-                copy(kind, pos).start()
+            if kind in LONG:
+                places = [START[kind] + j for j in range(START[kind + 1] - START[kind])]
+                ks = [slot_of_group(me, kind, 3, j) for j in range(len(places))]
+            else:
+                places = [START[kind] + 6 * i + j for j in range(6)]
+                ks = [slot_of_group(me, kind, j % 3, 2 * i + j // 3) for j in range(6)]
+            some(places, [scale[pl.ds(k, 1), :] for k in ks])
+            for pos, k in zip(places, ks):
+                pltpu.make_async_copy(ready.at[pos], out.at[k], sem).start()
             return carry
 
-        lax.fori_loop(0, (START[kind + 1] - START[kind]) // 4, one, 0)
+        if kind in LONG:
+            one(0, 0)
+        else:
+            lax.fori_loop(0, 2, one, 0)
 
     def store(pos, values, factor):
         ready[pos] = (values * jnp.concatenate([factor, factor], axis=1)).astype(jnp.bfloat16)
 
-    for kind in range(BESIDE_LONG):
-
-        def scaled(places):
-            for pos in places:
-                store(pos, x[pos].astype(jnp.float32), row(kind, pos))
-
-        in_fours(kind, scaled)
-
-    def whole(places):
+    def scaled(places, factors):
+        for pos, factor in zip(places, factors):
+            store(pos, x[pos].astype(jnp.float32), factor)
+
+    def whole(places, factors):
         halves = [
             jnp.dot(
                 left[:, pos - last].reshape(order, order), x[pos], preferred_element_type=jnp.float32
@@ -556,18 +563,15 @@
             jnp.dot(half, right[pos - last], preferred_element_type=jnp.float32)
             for pos, half in zip(places, halves)
         ]
-        for pos, precond in zip(places, preconds):
+        for pos, precond, factor in zip(places, preconds, factors):
             mean = jnp.sum(precond * precond, axis=(0, 1), keepdims=True) / float(order * order) + 1e-06
-            store(pos, precond, row(BESIDE_LONG, pos) / jnp.sqrt(mean))
-
-    in_fours(BESIDE_LONG, whole)
-    for kind in range(BESIDE_LONG + 1):
-
-        def settle(pos, carry):
-            copy(kind, pos).wait()
-            return carry
-
-        lax.fori_loop(START[kind], START[kind + 1], settle, 0)
+            store(pos, precond, factor / jnp.sqrt(mean))
+
+    for kind in (NEAR, NEAR_LONG, BESIDE, AWAY_LONG, AWAY):
+        in_groups(kind, scaled)
+    in_groups(BESIDE_LONG, whole)
+    in_groups(BESIDE_CROSS, scaled)
+    pltpu.make_async_copy(ready, out, sem).wait()
 
 
 def apply_scale(x, left, right, scale):
@@ -579,7 +583,7 @@
         out_specs=anywhere,
         scratch_shapes=[
             pltpu.VMEM(x.shape, jnp.bfloat16),
-            pltpu.SemaphoreType.DMA((x.shape[0],)),
+            pltpu.SemaphoreType.DMA,
         ],
         compiler_params=pltpu.CompilerParams(vmem_limit_bytes=24 * 2**20),
     )(x, left, right, scale)

time: 104 us -> 103 us (level)
  no operation moved by 1% of the time
where the time goes in v10:
time: 103 us
  Pallas kernels  103 us (100%)
    pallas_call x1, Pallas kernels, step(): pl.pallas_call(step_kernel, out_shape=(pltpu.VMEM((slots, *block), jnp.bf...  99.7 us
    pallas_call x1, Pallas kernels, apply_scale(): pl.pallas_call(scale_kernel, out_shape=jax.ShapeDtypeStruct(x.shape, jnp....  3.47 us

profile of v10, /device:TPU:1, one launch (start us, length us, event | category | flops | bytes accessed | tf_op | source)
XLA Modules:
  0.0 103.2 jit_solution(10638348943329715248)
XLA Ops:
  0.0 99.7 %shard_map.64 = (bf16[64,256,256]{2,1,0:T(8,128)(2,1)S(1)}, bf16[8,8,32,256]{3,2,1,0:T(8,128)(2,1)S(1)}, bf16[8,256,256]{2,1,0:T(8,128)(2,1)S(1)}, f32[64,128]{1,0:T(8,128)S(1)}) custom-call(s32[1,1024]{1,0:T(1,128)} %bitcast.10, bf16[32,256,256]{2,1,0:T(8,128)(2,1)} %grads_hbm.1, bf16[64,32,256]{2,1,0:T(8,128)(2,1)} %bitcast.9, ...), custom_call_target="tpu_custom_call" | custom-call | flops 4294967296 | bytes 400000000 | tf_op jit(solution)/shard_map/pallas_call | solution.py:477
  99.7 3.5 %shard_map.65 = bf16[64,256,256]{2,1,0:T(8,128)(2,1)} custom-call(bf16[64,256,256]{2,1,0:T(8,128)(2,1)S(1)} %get-tuple-element.9.x, bf16[8,8,32,256]{3,2,1,0:T(8,128)(2,1)S(1)} %get-tuple-element.10.left, bf16[8,256,256]{2,1,0:T(8,128)(2,1)S(1)} %get-tuple-element.11.right, f32[64,128]{1,0:T(8,128)S(1)} %get-tuple-element.12.scale), custom_call_target="tpu_custom_call" | custom-call | tf_op jit(solution)/shard_map/pallas_call | solution.py:579

commit v11 on v10

--- a/solution.py
+++ b/solution.py
@@ -390,11 +390,6 @@
         swap[h].start()
     absorb(BESIDE)
     pass_on(2, 2, 3)
-    done = [copy for group in (via, straight, onward, far, inside, strip) for copy in group.values()]
-    done += [passed[h, 1, part] for h, part in every] + [ahead[h, 0, part, 0] for h, part in every]
-    done += [ring_out(part, t, chunk) for t in range(2) for chunk in range(RING) for part in range(2)]
-    for copy in done:
-        copy.wait_send()
     for h, part in every:
         passed[h, 0, part].wait_recv()
     for dc in range(N_C):
@@ -427,9 +422,6 @@
 
     for dz in range(1, N_Z):
         tell(dz).start()
-    for chunk in range(RING):
-        for part in range(2):
-            ring_out(part, 2, chunk).wait_send()
     absorb(BESIDE_CROSS, adam=False)
     pass_on(3, 2)
     finish(AWAY)
@@ -459,11 +451,14 @@
     for dc in range(N_C):
         for h, part in every:
             ahead[h, 1, part, dc].wait_recv()
-    done = [passed[h, 0, part] for h, part in every] + [ahead[h, 0, part, 1] for h, part in every]
-    done += [ahead[h, 1, part, dc] for dc in range(N_C) for h, part in every]
-    done += [ring_out(part, 3, chunk) for chunk in range(RING) for part in range(2) if travels(part, 3, chunk)]
-    for copy in done:
-        copy.wait_send()
+    for group in (via, straight, onward, far, ahead, inside, passed, strip):
+        for copy in group.values():
+            copy.wait_send()
+    for t in range(4):
+        for chunk in range(RING):
+            for part in range(2):
+                if travels(part, t, chunk):
+                    ring_out(part, t, chunk).wait_send()
 
 
 def step(owner, grads, left, right, mone, mtwo):

time: 103 us -> 104 us (level)
  no operation moved by 1% of the time
where the time goes in v11:
time: 104 us; the launch traced here: 103 us
  Pallas kernels  103 us (99%)
    pallas_call x1, Pallas kernels, step(): pl.pallas_call(step_kernel, out_shape=(pltpu.VMEM((slots, *block), jnp.bf...  99.8 us
    pallas_call x1, Pallas kernels, apply_scale(): pl.pallas_call(scale_kernel, out_shape=jax.ShapeDtypeStruct(x.shape, jnp....  3.47 us

profile of v11, /device:TPU:1, one launch (start us, length us, event | category | flops | bytes accessed | tf_op | source)
XLA Modules:
  0.0 103.3 jit_solution(6805702303660006849)
XLA Ops:
  0.0 99.8 %shard_map.64 = (bf16[64,256,256]{2,1,0:T(8,128)(2,1)S(1)}, bf16[8,8,32,256]{3,2,1,0:T(8,128)(2,1)S(1)}, bf16[8,256,256]{2,1,0:T(8,128)(2,1)S(1)}, f32[64,128]{1,0:T(8,128)S(1)}) custom-call(s32[1,1024]{1,0:T(1,128)} %bitcast.10, bf16[32,256,256]{2,1,0:T(8,128)(2,1)} %grads_hbm.1, bf16[64,32,256]{2,1,0:T(8,128)(2,1)} %bitcast.9, ...), custom_call_target="tpu_custom_call" | custom-call | flops 4294967296 | bytes 400000000 | tf_op jit(solution)/shard_map/pallas_call | solution.py:472
  99.8 3.5 %shard_map.65 = bf16[64,256,256]{2,1,0:T(8,128)(2,1)} custom-call(bf16[64,256,256]{2,1,0:T(8,128)(2,1)S(1)} %get-tuple-element.9.x, bf16[8,8,32,256]{3,2,1,0:T(8,128)(2,1)S(1)} %get-tuple-element.10.left, bf16[8,256,256]{2,1,0:T(8,128)(2,1)S(1)} %get-tuple-element.11.right, f32[64,128]{1,0:T(8,128)S(1)} %get-tuple-element.12.scale), custom_call_target="tpu_custom_call" | custom-call | tf_op jit(solution)/shard_map/pallas_call | solution.py:574
